TPU v7x, 128 devices: a whole 4x4x4 slice. The times are simulated.
128 devices in a mesh: grp: 8 (over z_hi, y), dev: 16 (over x, z_lo, core).
Axes of the slice: x: 4, y: 4, z: 4 (z_hi: 2, z_lo: 2; z = z_hi * 2 + z_lo), core: 2. Of those that a mesh axis runs over, the one named last changes fastest.
Arguments:
- gas_velocity: float32 [8, 3, 128, 128, 128], P('grp', None, 'dev'), may hold values from -6 to 6
- parcel_velocity: float32 [8, 3, 64, 16384], P('grp', None, None, 'dev'), may hold values from -6 to 6
- parcel_cell: int32 [8, 64, 16384], P('grp', None, 'dev'), may hold values from 0 to 127
- block_fill: int32 [8, 16384], P('grp', 'dev'), may hold values from 0 to 64
- relax_rate: float32 [8, 64, 16384], P('grp', None, 'dev'), may hold values from 0.1 to 10
- parcel_mass: float32 [8, 64, 16384], P('grp', None, 'dev'), may hold values from 0.1 to 1
- sample_blocks: bfloat16 [5632, 16, 256], P(('grp', 'dev')), may hold values from -6 to 6
- learner_ids: int32 [5632], P(('grp', 'dev')), may hold values from 0 to 47, as said below
- master_weights: float32 [10240, 128], P('dev'), may hold values from -2 to 2
- first_moment: float32 [10240, 128], P('dev'), may hold values from -6 to 6
- second_moment: float32 [10240, 128], P('dev'), may hold values from 1 to 30
Outputs:
- gas_out: float32 [8, 3, 128, 128, 128], P('grp', None, 'dev')
- parcel_out: float32 [8, 3, 64, 16384], P('grp', None, None, 'dev')
- master_out: float32 [10240, 128], P('dev')
- first_out: float32 [10240, 128], P('dev')
- second_out: float32 [10240, 128], P('dev')
Inputs may be any that keep to these rules, and one draw needn't show every extreme that they name: `learner_ids`: each device's 44 blocks go to 44 different learners; every learner receives at least one block and at most 128, and some learner receives exactly 128.
All inputs are finite; a program needn't handle non-finite values.
Results may differ from a plain program's by a relative error of at most 0.0004.
The roundings to bfloat16 on the way count: a program that leaves them out, or rounds other values in their place, can miss the bound.
Values may be sent and summed in bfloat16 or wider, within the bound.
A program may use at most 128 MiB of HBM per device.

v0:
```python
import math

import jax
import jax.numpy as jnp
from jax import lax
from jax.sharding import PartitionSpec as P

CB = 128
SUB = 2
F_IN = 128
HID = 1024
F_OUT = 128


KAPPA = 0.15
BETA_ONE = 0.9
BETA_TWO = 0.95
ADAM_EPS = 1e-08
LEARN_RATE = 0.001
ADAM_STEP = 10


def extended_2(cells, sides, width):
    for axis, dim in sides:
        count = lax.axis_size(axis)
        head = lax.slice_in_dim(cells, 0, width, axis=dim)
        tail = lax.slice_in_dim(cells, cells.shape[dim] - width, cells.shape[dim], axis=dim)
        cells = jnp.concatenate(
            [
                lax.ppermute(tail, axis, [(i, (i + 1) % count) for i in range(count)]),
                cells,
                lax.ppermute(head, axis, [((i + 1) % count, i) for i in range(count)]),
            ],
            axis=dim,
        )
    return cells


def walls_sum(gas_field):
    padded = jnp.pad(gas_field, [(0, 0), (0, 0), (0, 0), (1, 1), (1, 1)])
    return (
        padded[:, :, :, 2:, 1:-1]
        + padded[:, :, :, :-2, 1:-1]
        + padded[:, :, :, 1:-1, 2:]
        + padded[:, :, :, 1:-1, :-2]
    )


def diffuse(gas_field, lower_side, upper_side):
    return gas_field + KAPPA * (lower_side + upper_side + walls_sum(gas_field) - 6.0 * gas_field)


def gas_rims(gas_field):
    return extended_2(gas_field, (("dev", 2),), 1)


def silu_slope(argument):
    sigmoid_value = jax.nn.sigmoid(argument)
    return sigmoid_value * (1.0 + argument * (1.0 - sigmoid_value))


def contract_rows(left_side, right_side):
    return lax.dot_general(
        left_side, right_side, (((0,), (0,)), ((), ())), preferred_element_type=jnp.float32
    )


def contract_columns(left_side, right_side):
    return lax.dot_general(
        left_side, right_side, (((1,), (1,)), ((), ())), preferred_element_type=jnp.float32
    )


def model_grads(full_weights, features, targets, row_scale):
    flattened = full_weights.reshape(-1)
    first_end = F_IN * HID
    second_end = first_end + HID * HID
    w_first = flattened[:first_end].reshape(F_IN, HID)
    w_second = flattened[first_end:second_end].reshape(HID, HID)
    w_third = flattened[second_end:].reshape(HID, F_OUT)
    pre_first = jnp.dot(features, w_first, preferred_element_type=jnp.float32)
    act_first = jax.nn.silu(pre_first).astype(jnp.bfloat16)
    pre_second = jnp.dot(act_first, w_second, preferred_element_type=jnp.float32)
    act_second = jax.nn.silu(pre_second).astype(jnp.bfloat16)
    predicted = jnp.dot(act_second, w_third, preferred_element_type=jnp.float32)
    error_scaled = ((predicted - targets.astype(jnp.float32)) * row_scale[:, None]).astype(
        jnp.bfloat16
    )
    grad_third = contract_rows(act_second, error_scaled)
    back_second = (contract_columns(error_scaled, w_third) * silu_slope(pre_second)).astype(
        jnp.bfloat16
    )
    grad_second = contract_rows(act_first, back_second)
    back_first = (contract_columns(back_second, w_second) * silu_slope(pre_first)).astype(
        jnp.bfloat16
    )
    grad_first = contract_rows(features, back_first)
    joined = jnp.concatenate(
        [grad_first.reshape(-1), grad_second.reshape(-1), grad_third.reshape(-1)]
    )
    return joined.reshape(full_weights.shape[0], full_weights.shape[1])


def adam_update(weights, moment_one, moment_two, gradient):
    first_new = BETA_ONE * moment_one + (1.0 - BETA_ONE) * gradient
    second_new = BETA_TWO * moment_two + (1.0 - BETA_TWO) * gradient * gradient
    first_hat = first_new / (1.0 - BETA_ONE**ADAM_STEP)
    second_hat = second_new / (1.0 - BETA_TWO**ADAM_STEP)
    updated = weights - LEARN_RATE * first_hat / (jnp.sqrt(second_hat) + ADAM_EPS)
    return (updated, first_new, second_new)


def shards(
    gas_velocity,
    parcel_velocity,
    parcel_cell,
    block_fill,
    relax_rate,
    parcel_mass,
    sample_blocks,
    learner_ids,
    master_weights,
    first_moment,
    second_moment,
):
    groups = lax.axis_size("grp")
    slab_total = lax.axis_size("dev")
    sim_groups = 5 * groups // 8
    learner_groups = groups - sim_groups
    group_index = lax.axis_index("grp")
    slab_index = lax.axis_index("dev")
    quarter_learner = (group_index == groups // 4) & (learner_groups >= 3)
    is_learner = (group_index == 0) | (group_index == groups // 2) | quarter_learner
    in_evolution = jnp.logical_not(is_learner)
    extended = gas_rims(gas_velocity)
    lower_side = extended[:, :, :-2]
    upper_side = extended[:, :, 2:]
    slab_cells = gas_velocity.shape[2] * gas_velocity.shape[3] * gas_velocity.shape[4]
    block_count = slab_cells // CB
    smoothed = (0.5 * gas_velocity + 0.25 * (lower_side + upper_side)).reshape(3, block_count, CB)
    group_size = math.gcd(block_count, 128)
    group_total = block_count // group_size
    slot_total = parcel_cell.shape[1]
    cell_rows = parcel_cell[0]
    velocity_rows = parcel_velocity[0]
    rate_rows = relax_rate[0]
    mass_rows = parcel_mass[0]
    fill_rows = block_fill[0]
    columns = jnp.arange(CB, dtype=jnp.int32)
    slot_numbers = jnp.arange(slot_total, dtype=jnp.int32)

    def block_group(number):
        block_start = number * group_size
        index_part = lax.dynamic_slice_in_dim(cell_rows, block_start, group_size, 1)
        velocity_part = lax.dynamic_slice_in_dim(velocity_rows, block_start, group_size, 2)
        rate_part = lax.dynamic_slice_in_dim(rate_rows, block_start, group_size, 1)
        mass_part = lax.dynamic_slice_in_dim(mass_rows, block_start, group_size, 1)
        fill_part = lax.dynamic_slice_in_dim(fill_rows, block_start, group_size, 0)
        gas_part = lax.dynamic_slice_in_dim(smoothed, block_start, group_size, 1)
        onehot = (index_part[:, :, None] == columns).astype(jnp.float32)
        live_slots = slot_numbers[:, None] < fill_part[None, :]
        gas_at = jnp.einsum("pbc,kbc->kpb", onehot, gas_part, precision=lax.Precision.HIGHEST)
        relaxed = (velocity_part + rate_part * gas_at) / (1.0 + rate_part)
        moved_velocity = jnp.where(live_slots, relaxed, velocity_part)
        handed = jnp.where(live_slots, mass_part * (velocity_part - relaxed), 0.0)
        deposit = jnp.einsum("pbc,kpb->kbc", onehot, handed, precision=lax.Precision.HIGHEST)
        return (moved_velocity, deposit)

    moved_all, deposit_all = lax.map(block_group, jnp.arange(group_total, dtype=jnp.int32))
    moved_all = moved_all.transpose(1, 2, 0, 3).reshape(parcel_velocity.shape)
    deposit_field = deposit_all.transpose(1, 0, 2, 3).reshape(gas_velocity.shape)
    deposit_ext = extended_2(deposit_field.astype(jnp.bfloat16), (("dev", 2),), 1).astype(
        deposit_field.dtype
    )
    source = 0.5 * deposit_field + 0.25 * (deposit_ext[:, :, :-2] + deposit_ext[:, :, 2:])
    gas_field = gas_velocity
    for substep in range(SUB):
        if substep > 0:
            extended = gas_rims(gas_field)
            lower_side = extended[:, :, :-2]
            upper_side = extended[:, :, 2:]
        gas_field = diffuse(gas_field, lower_side, upper_side)
        if substep == 0:
            gas_field = gas_field + source
    gas_out = jnp.where(in_evolution, gas_field, gas_velocity)
    parcel_out = jnp.where(in_evolution, moved_all, parcel_velocity)
    block_rows = sample_blocks.shape[1]
    total_width = sample_blocks.shape[2]
    senders = groups * slab_total
    learner_rank = learner_ids // slab_total
    target_group = jnp.where(
        learner_rank == 0, 0, jnp.where(learner_rank == 1, groups // 2, groups // 4)
    )
    target_slot = target_group * slab_total + learner_ids % slab_total
    sender_slots = jnp.arange(senders, dtype=jnp.int32)
    routing = sender_slots[:, None] == target_slot[None, :]
    outgoing = jnp.einsum(
        "sn,nrf->srf",
        routing.astype(jnp.bfloat16),
        sample_blocks,
        preferred_element_type=jnp.float32,
    ).astype(jnp.bfloat16)
    live_flags = routing.astype(jnp.int32).sum(axis=1)
    received, received_flags = (
        lax.all_to_all(outgoing, ("grp", "dev"), split_axis=0, concat_axis=0, tiled=True),
        lax.all_to_all(live_flags, ("grp", "dev"), split_axis=0, concat_axis=0, tiled=True),
    )
    full_weights = lax.all_gather(master_weights.astype(jnp.bfloat16), "dev", axis=0, tiled=True)

    def train_branch(operands):
        arrived, arrived_flags, weights_rounded = operands
        block_total = jnp.maximum(arrived_flags.sum(), 1)
        row_live = arrived_flags == 1
        block_scale = row_live.astype(jnp.float32) / block_total.astype(jnp.float32)
        row_scale = jnp.repeat(block_scale, block_rows)
        flat_rows = arrived.reshape(-1, total_width)
        return model_grads(weights_rounded, flat_rows[:, :F_IN], flat_rows[:, F_IN:], row_scale)

    def other_branch(operands):
        return jnp.zeros(operands[2].shape, jnp.float32)

    gradient = lax.cond(
        is_learner, train_branch, other_branch, (received, received_flags, full_weights)
    )
    shard_rows = master_weights.shape[0]
    complete = lax.psum(gradient, ("grp", "dev"))
    summed = lax.dynamic_slice_in_dim(complete, slab_index * shard_rows, shard_rows, 0)
    master_out, first_out, second_out = adam_update(
        master_weights, first_moment, second_moment, summed
    )
    return (gas_out, parcel_out, master_out, first_out, second_out)


def solution(mesh):
    placed = (
        P("grp", None, "dev", None, None),
        P("grp", None, None, "dev"),
        P("grp", None, "dev"),
        P("grp", "dev"),
        P("grp", None, "dev"),
        P("grp", None, "dev"),
        P(("grp", "dev"), None, None),
        P(("grp", "dev")),
        P("dev", None),
        P("dev", None),
        P("dev", None),
    )
    return jax.shard_map(
        shards,
        mesh=mesh,
        in_specs=placed,
        out_specs=(
            P("grp", None, "dev", None, None),
            P("grp", None, None, "dev"),
            P("dev", None),
            P("dev", None),
            P("dev", None),
        ),
        check_vma=False,
    )
```

profile of v0, /device:TPU:0, one launch (start us, length us, event | category | flops | bytes accessed | tf_op | source)
XLA Modules:
  0.0 288.6 jit_solution(18150037153406024093)
XLA Ops:
  7.2 1.7 convert_element_type.65
  10.5 11.1 %all-to-all-start.1 = ((s32[128,1,1]{2,1,0:T(1,128)}), s32[128,1,1]{2,1,0:T(1,128)S(1)}, u32[]{:S(2)}, u32[]{:S(2)}) async-start(s32[128,1,1]{2,1,0:T(1,128)} %copy.48), calls=%async_computation.1 | async-start | bytes 131072 | tf_op jit(solution)/shard_map/all_to_all | solution.py:206
  22.2 1.6 copy.47
  23.8 6.9 %all-to-all-done.1 = s32[128,1,1]{2,1,0:T(1,128)S(1)} async-done(((s32[128,1,1]{2,1,0:T(1,128)}), s32[128,1,1]{2,1,0:T(1,128)S(1)}, u32[]{:S(2)}, u32[]{:S(2)}) %all-to-all-start.1) | async-done | bytes 544 | tf_op jit(solution)/shard_map/all_to_all | solution.py:206
  30.7 5.8 %all-to-all-start = ((bf16[128,16,256]{2,1,0:T(8,128)(2,1)}), bf16[128,16,256]{2,1,0:T(8,128)(2,1)}, u32[]{:S(2)}, u32[]{:S(2)}) async-start(bf16[128,16,256]{2,1,0:T(8,128)(2,1)} %copy.47), calls=%async_computation | async-start | bytes 2097152 | tf_op jit(solution)/shard_map/all_to_all | solution.py:205
  37.3 2.9 %collective-permute-start.1 = (f32[1,3,1,128,128]{4,3,2,1,0:T(8,128)}, f32[1,3,1,128,128]{4,3,2,1,0:T(8,128)S(1)}, u32[]{:S(2)}, u32[]{:S(2)}) collective-permute-start(f32[1,3,1,128,128]{4,3,2,1,0:T(8,128)} %get-tuple-element.178), channel_id=1, source_target_pairs={{1,0},{2,1},{3,2},{4,3},{5,4},{6,5},{7,6},{8,7},{9,8},{10,9},{11,1... | collective-permute-start | bytes 589832 | tf_op jit(solution)/shard_map/ppermute | solution.py:32
  40.2 2.7 copy.38
  43.0 1.9 copy.39
  44.9 2.0 copy.40
  46.9 2.0 copy.41
  48.9 2.8 collective-permute-done
  51.7 2.3 fusion.56
  54.0 4.0 %all-to-all-done = bf16[128,16,256]{2,1,0:T(8,128)(2,1)} async-done(((bf16[128,16,256]{2,1,0:T(8,128)(2,1)}), bf16[128,16,256]{2,1,0:T(8,128)(2,1)}, u32[]{:S(2)}, u32[]{:S(2)}) %all-to-all-start) | async-done | bytes 1048608 | tf_op jit(solution)/shard_map/all_to_all | solution.py:205
  58.0 1.1 all-gather.2.cloned.1.call-done
  59.2 63.4 %conditional.1 = (f32[10240,128]{1,0:T(8,128)}) conditional(s32[]{:T(128)} %convert_element_type.63, () %tuple.19, (bf16[128,16,256]{2,1,0:T(8,128)(2,1)}, bf16[10240,128]{1,0:T(8,128)(2,1)}, s32[128,1,1]{2,1,0:T(1,128)S(1)}) %tuple.66), branch_computations={%region_3.4_spmd, %region_4.6_spmd} | conditional | flops 15642132480 | bytes 253529344 | solution.py:222
  59.2 3.1 %slice.59 = bf16[8192,128]{1,0:T(8,128)(2,1)} slice(bf16[10240,128]{1,0:T(8,128)(2,1)} %get-tuple-element.72), slice={[1024:9216], [0:128]} | slice | bytes 4194304 | tf_op jit(solution)/shard_map/cond/branch_1_fun/slice | solution.py:79
  62.2 4.2 %reshape.105 = bf16[1024,1024]{1,0:T(8,128)(2,1)} reshape(bf16[8192,128]{1,0:T(8,128)(2,1)} %slice.59) | data formatting | bytes 4194304 | tf_op jit(solution)/shard_map/cond/branch_1_fun/reshape | solution.py:79
  66.4 1.7 slice.58
  68.1 1.1 reshape.104
  69.2 2.4 fusion.9
  71.6 8.6 %multiply_convert_fusion.2 = (bf16[2048,1024]{1,0:T(8,128)(2,1)}, f32[2048,1024]{1,0:T(8,128)}) fusion(bf16[1024,1024]{1,0:T(8,128)(2,1)S(1)} %copy-done.8, f32[2048,1024]{1,0:T(8,128)S(1)} %fusion.9), kind=kOutput, calls=%fused_computation.5 | convolution fusion | flops 4315938816 | bytes 23068672 | tf_op jit(solution)/shard_map/cond/branch_1_fun/dot_general | solution.py:83
  81.9 3.8 %fusion.5 = bf16[2048,128]{1,0:T(8,128)(2,1)S(1)} fusion(bf16[2048,1024]{1,0:T(8,128)(2,1)} %get-tuple-element.170, bf16[2048,256]{1,0:T(8,128)(2,1)} %bitcast, f32[2048]{0:T(1024)S(1)} %mul.95, bf16[10240,128]{1,0:T(8,128)(2,1)} %get-tuple-element.72), kind=kOutput, calls=%fused_computation.12 | convolution fusion | flops 537919488 | bytes 5513216 | tf_op jit(solution)/shard_map/cond/branch_1_fun/dot_general | solution.py:85
  85.7 2.1 convolution_bitcast_fusion
  88.1 4.9 %multiply_convert_fusion.1 = bf16[2048,1024]{1,0:T(8,128)(2,1)S(1)} fusion(f32[2048,1024]{1,0:T(8,128)S(1)} %copy-done.16, bf16[2048,128]{1,0:T(8,128)(2,1)S(1)} %fusion.5, bf16[10240,128]{1,0:T(8,128)(2,1)} %get-tuple-element.72), kind=kOutput, calls=%fused_computation.4 | convolution fusion | flops 555745280 | bytes 13369344 | tf_op jit(solution)/shard_map/cond/branch_1_fun/dot_general | solution.py:69
  93.0 4.7 %convolution_bitcast_fusion.1 = f32[128,8,8,128]{3,2,1,0:T(8,128)S(1)} fusion(bf16[2048,1024]{1,0:T(8,128)(2,1)S(1)} %multiply_convert_fusion.1, f32[2048,1024]{1,0:T(8,128)S(1)} %bitcast.66), kind=kOutput, calls=%fused_computation.13 | convolution fusion | flops 4305453056 | bytes 16777216 | tf_op jit(solution)/shard_map/cond/branch_1_fun/dot_general | solution.py:63
  97.8 3.1 %copy.58 = f32[128,8,8,128]{3,1,2,0:T(8,128)} copy(f32[128,8,8,128]{3,2,1,0:T(8,128)S(1)} %convolution_bitcast_fusion.1) | data formatting | bytes 8388608 | tf_op jit(solution)/shard_map/cond
  100.8 13.8 %fusion.7 = f32[128,1024]{0,1:T(8,128)} fusion(f32[2048,1024]{1,0:T(8,128)} %copy-done.2, bf16[2048,1024]{1,0:T(8,128)(2,1)} %copy-done.17, bf16[1024,1024]{1,0:T(8,128)(2,1)} %reshape.105, bf16[2048,256]{1,0:T(8,128)(2,1)} %bitcast), kind=kOutput, calls=%fused_computation.15 | convolution fusion | flops 4850712576 | bytes 15728640 | tf_op jit(solution)/shard_map/cond/branch_1_fun/dot_general | solution.py:63
  114.7 2.0 copy.37
  116.7 1.1 copy.57
  117.8 4.7 %maximum_bitcast_fusion = f32[10240,128]{1,0:T(8,128)} fusion(f32[131072]{0:T(1024)} %convolution_bitcast_fusion, f32[1048576]{0:T(1024)} %bitcast.67, f32[131072]{0:T(1024)S(1)} %bitcast.69), kind=kLoop, calls=%fused_computation.9 | loop fusion | flops 2621440 | bytes 10485760 | tf_op jit(solution)/shard_map/cond/branch_1_fun/reshape | solution.py:101
  122.6 110.4 %while.13 = (s32[]{:T(128)}, f32[8,3,64,128]{2,1,3,0:T(4,128)}, f32[8,3,128,128]{3,2,0,1:T(8,128)S(1)}, s32[8]{0:T(128)S(1)}, s32[1024]{0:T(1024)}, /*index=5*/f...) while((s32[]{:T(128)}, f32[8,3,64,128]{2,1,3,0:T(4,128)}, ...), condition=%wide.region_1.2_spmd.clone, body=%wide.region_0.1_spmd.clone.sunk | while | flops 77783040 | bytes 2647783 | solution.py:169
  126.5 0.9 constant_dynamic-slice_fusion.8
  127.4 5.5 %bitcast_dynamic-update-slice_fusion.2 = (f32[8,3,64,128]{2,1,3,0:T(4,128)}, f32[3,64,128]{1,0,2:T(4,128)S(1)}) fusion(f32[8,3,64,128]{2,1,3,0:T(4,128)} %get-tuple-element.267, s32[]{:T(128)S(6)} %copy.75, f32[3,64,1024]{1,0,2:T(4,128)} %get-tuple-element.285, s32[]{:T(128)S(6)} %select_n.93, pred[64,128]{0,1:T(8,128)(4,1)S(1)} %iota_compare_fusion.18, ...), kind=kOutput, calls=%fused_computation.36.clone.1 | convolution fusion | flops 38895616 | bytes 925704 | tf_op jit(solution)/shard_map/while/body/eval_jaxpr/pbc,kbc->kpb/dot_general | solution.py:162
  132.9 3.4 %fusion.80 = f32[1,3,128,128]{3,1,2,0:T(4,128)S(1)} fusion(s32[64,128]{0,1:T(8,128)S(1)} %constant_dynamic-slice_fusion.7, f32[3,64,128]{1,0,2:T(4,128)S(1)} %get-tuple-element.250, f32[3,64,1024]{1,0,2:T(4,128)} %get-tuple-element.285, s32[]{:T(128)S(6)} %select_n.93, f32[64,128]{0,1:T(8,128)S(1)} %get-tuple-element.251, ...), kind=kOutput, calls=%fused_computation.34.clone.1 | convolution fusion | flops 38871040 | bytes 630788 | tf_op jit(solution)/shard_map/while/body/eval_jaxpr/pbc,kpb->kbc/dot_general | solution.py:166
  140.3 1.0 constant_dynamic-slice_fusion.8
  141.2 5.5 %bitcast_dynamic-update-slice_fusion.2 = (f32[8,3,64,128]{2,1,3,0:T(4,128)}, f32[3,64,128]{1,0,2:T(4,128)S(1)}) fusion(f32[8,3,64,128]{2,1,3,0:T(4,128)} %get-tuple-element.267, s32[]{:T(128)S(6)} %copy.75, f32[3,64,1024]{1,0,2:T(4,128)} %get-tuple-element.285, s32[]{:T(128)S(6)} %select_n.93, pred[64,128]{0,1:T(8,128)(4,1)S(1)} %iota_compare_fusion.18, ...), kind=kOutput, calls=%fused_computation.36.clone.1 | convolution fusion | flops 38895616 | bytes 925704 | tf_op jit(solution)/shard_map/while/body/eval_jaxpr/pbc,kbc->kpb/dot_general | solution.py:162
  146.7 3.4 %fusion.80 = f32[1,3,128,128]{3,1,2,0:T(4,128)S(1)} fusion(s32[64,128]{0,1:T(8,128)S(1)} %constant_dynamic-slice_fusion.7, f32[3,64,128]{1,0,2:T(4,128)S(1)} %get-tuple-element.250, f32[3,64,1024]{1,0,2:T(4,128)} %get-tuple-element.285, s32[]{:T(128)S(6)} %select_n.93, f32[64,128]{0,1:T(8,128)S(1)} %get-tuple-element.251, ...), kind=kOutput, calls=%fused_computation.34.clone.1 | convolution fusion | flops 38871040 | bytes 630788 | tf_op jit(solution)/shard_map/while/body/eval_jaxpr/pbc,kpb->kbc/dot_general | solution.py:166
  154.1 0.9 constant_dynamic-slice_fusion.8
  155.0 5.5 %bitcast_dynamic-update-slice_fusion.2 = (f32[8,3,64,128]{2,1,3,0:T(4,128)}, f32[3,64,128]{1,0,2:T(4,128)S(1)}) fusion(f32[8,3,64,128]{2,1,3,0:T(4,128)} %get-tuple-element.267, s32[]{:T(128)S(6)} %copy.75, f32[3,64,1024]{1,0,2:T(4,128)} %get-tuple-element.285, s32[]{:T(128)S(6)} %select_n.93, pred[64,128]{0,1:T(8,128)(4,1)S(1)} %iota_compare_fusion.18, ...), kind=kOutput, calls=%fused_computation.36.clone.1 | convolution fusion | flops 38895616 | bytes 925704 | tf_op jit(solution)/shard_map/while/body/eval_jaxpr/pbc,kbc->kpb/dot_general | solution.py:162
  160.5 3.4 %fusion.80 = f32[1,3,128,128]{3,1,2,0:T(4,128)S(1)} fusion(s32[64,128]{0,1:T(8,128)S(1)} %constant_dynamic-slice_fusion.7, f32[3,64,128]{1,0,2:T(4,128)S(1)} %get-tuple-element.250, f32[3,64,1024]{1,0,2:T(4,128)} %get-tuple-element.285, s32[]{:T(128)S(6)} %select_n.93, f32[64,128]{0,1:T(8,128)S(1)} %get-tuple-element.251, ...), kind=kOutput, calls=%fused_computation.34.clone.1 | convolution fusion | flops 38871040 | bytes 630788 | tf_op jit(solution)/shard_map/while/body/eval_jaxpr/pbc,kpb->kbc/dot_general | solution.py:166
  167.9 0.9 constant_dynamic-slice_fusion.8
  168.8 5.5 %bitcast_dynamic-update-slice_fusion.2 = (f32[8,3,64,128]{2,1,3,0:T(4,128)}, f32[3,64,128]{1,0,2:T(4,128)S(1)}) fusion(f32[8,3,64,128]{2,1,3,0:T(4,128)} %get-tuple-element.267, s32[]{:T(128)S(6)} %copy.75, f32[3,64,1024]{1,0,2:T(4,128)} %get-tuple-element.285, s32[]{:T(128)S(6)} %select_n.93, pred[64,128]{0,1:T(8,128)(4,1)S(1)} %iota_compare_fusion.18, ...), kind=kOutput, calls=%fused_computation.36.clone.1 | convolution fusion | flops 38895616 | bytes 925704 | tf_op jit(solution)/shard_map/while/body/eval_jaxpr/pbc,kbc->kpb/dot_general | solution.py:162
  174.3 3.4 %fusion.80 = f32[1,3,128,128]{3,1,2,0:T(4,128)S(1)} fusion(s32[64,128]{0,1:T(8,128)S(1)} %constant_dynamic-slice_fusion.7, f32[3,64,128]{1,0,2:T(4,128)S(1)} %get-tuple-element.250, f32[3,64,1024]{1,0,2:T(4,128)} %get-tuple-element.285, s32[]{:T(128)S(6)} %select_n.93, f32[64,128]{0,1:T(8,128)S(1)} %get-tuple-element.251, ...), kind=kOutput, calls=%fused_computation.34.clone.1 | convolution fusion | flops 38871040 | bytes 630788 | tf_op jit(solution)/shard_map/while/body/eval_jaxpr/pbc,kpb->kbc/dot_general | solution.py:166
  181.7 0.9 constant_dynamic-slice_fusion.8
  182.6 5.5 %bitcast_dynamic-update-slice_fusion.2 = (f32[8,3,64,128]{2,1,3,0:T(4,128)}, f32[3,64,128]{1,0,2:T(4,128)S(1)}) fusion(f32[8,3,64,128]{2,1,3,0:T(4,128)} %get-tuple-element.267, s32[]{:T(128)S(6)} %copy.75, f32[3,64,1024]{1,0,2:T(4,128)} %get-tuple-element.285, s32[]{:T(128)S(6)} %select_n.93, pred[64,128]{0,1:T(8,128)(4,1)S(1)} %iota_compare_fusion.18, ...), kind=kOutput, calls=%fused_computation.36.clone.1 | convolution fusion | flops 38895616 | bytes 925704 | tf_op jit(solution)/shard_map/while/body/eval_jaxpr/pbc,kbc->kpb/dot_general | solution.py:162
  188.1 3.4 %fusion.80 = f32[1,3,128,128]{3,1,2,0:T(4,128)S(1)} fusion(s32[64,128]{0,1:T(8,128)S(1)} %constant_dynamic-slice_fusion.7, f32[3,64,128]{1,0,2:T(4,128)S(1)} %get-tuple-element.250, f32[3,64,1024]{1,0,2:T(4,128)} %get-tuple-element.285, s32[]{:T(128)S(6)} %select_n.93, f32[64,128]{0,1:T(8,128)S(1)} %get-tuple-element.251, ...), kind=kOutput, calls=%fused_computation.34.clone.1 | convolution fusion | flops 38871040 | bytes 630788 | tf_op jit(solution)/shard_map/while/body/eval_jaxpr/pbc,kpb->kbc/dot_general | solution.py:166
  195.5 0.9 constant_dynamic-slice_fusion.8
  196.4 5.5 %bitcast_dynamic-update-slice_fusion.2 = (f32[8,3,64,128]{2,1,3,0:T(4,128)}, f32[3,64,128]{1,0,2:T(4,128)S(1)}) fusion(f32[8,3,64,128]{2,1,3,0:T(4,128)} %get-tuple-element.267, s32[]{:T(128)S(6)} %copy.75, f32[3,64,1024]{1,0,2:T(4,128)} %get-tuple-element.285, s32[]{:T(128)S(6)} %select_n.93, pred[64,128]{0,1:T(8,128)(4,1)S(1)} %iota_compare_fusion.18, ...), kind=kOutput, calls=%fused_computation.36.clone.1 | convolution fusion | flops 38895616 | bytes 925704 | tf_op jit(solution)/shard_map/while/body/eval_jaxpr/pbc,kbc->kpb/dot_general | solution.py:162
  201.9 3.4 %fusion.80 = f32[1,3,128,128]{3,1,2,0:T(4,128)S(1)} fusion(s32[64,128]{0,1:T(8,128)S(1)} %constant_dynamic-slice_fusion.7, f32[3,64,128]{1,0,2:T(4,128)S(1)} %get-tuple-element.250, f32[3,64,1024]{1,0,2:T(4,128)} %get-tuple-element.285, s32[]{:T(128)S(6)} %select_n.93, f32[64,128]{0,1:T(8,128)S(1)} %get-tuple-element.251, ...), kind=kOutput, calls=%fused_computation.34.clone.1 | convolution fusion | flops 38871040 | bytes 630788 | tf_op jit(solution)/shard_map/while/body/eval_jaxpr/pbc,kpb->kbc/dot_general | solution.py:166
  210.2 5.5 %bitcast_dynamic-update-slice_fusion.2 = (f32[8,3,64,128]{2,1,3,0:T(4,128)}, f32[3,64,128]{1,0,2:T(4,128)S(1)}) fusion(f32[8,3,64,128]{2,1,3,0:T(4,128)} %get-tuple-element.267, s32[]{:T(128)S(6)} %copy.75, f32[3,64,1024]{1,0,2:T(4,128)} %get-tuple-element.285, s32[]{:T(128)S(6)} %select_n.93, pred[64,128]{0,1:T(8,128)(4,1)S(1)} %iota_compare_fusion.18, ...), kind=kOutput, calls=%fused_computation.36.clone.1 | convolution fusion | flops 38895616 | bytes 925704 | tf_op jit(solution)/shard_map/while/body/eval_jaxpr/pbc,kbc->kpb/dot_general | solution.py:162
  215.7 3.4 %fusion.80 = f32[1,3,128,128]{3,1,2,0:T(4,128)S(1)} fusion(s32[64,128]{0,1:T(8,128)S(1)} %constant_dynamic-slice_fusion.7, f32[3,64,128]{1,0,2:T(4,128)S(1)} %get-tuple-element.250, f32[3,64,1024]{1,0,2:T(4,128)} %get-tuple-element.285, s32[]{:T(128)S(6)} %select_n.93, f32[64,128]{0,1:T(8,128)S(1)} %get-tuple-element.251, ...), kind=kOutput, calls=%fused_computation.34.clone.1 | convolution fusion | flops 38871040 | bytes 630788 | tf_op jit(solution)/shard_map/while/body/eval_jaxpr/pbc,kpb->kbc/dot_general | solution.py:166
  224.0 5.5 %bitcast_dynamic-update-slice_fusion.2 = (f32[8,3,64,128]{2,1,3,0:T(4,128)}, f32[3,64,128]{1,0,2:T(4,128)S(1)}) fusion(f32[8,3,64,128]{2,1,3,0:T(4,128)} %get-tuple-element.267, s32[]{:T(128)S(6)} %copy.75, f32[3,64,1024]{1,0,2:T(4,128)} %get-tuple-element.285, s32[]{:T(128)S(6)} %select_n.93, pred[64,128]{0,1:T(8,128)(4,1)S(1)} %iota_compare_fusion.18, ...), kind=kOutput, calls=%fused_computation.36.clone.1 | convolution fusion | flops 38895616 | bytes 925704 | tf_op jit(solution)/shard_map/while/body/eval_jaxpr/pbc,kbc->kpb/dot_general | solution.py:162
  229.5 3.5 %fusion.80 = f32[1,3,128,128]{3,1,2,0:T(4,128)S(1)} fusion(s32[64,128]{0,1:T(8,128)S(1)} %constant_dynamic-slice_fusion.7, f32[3,64,128]{1,0,2:T(4,128)S(1)} %get-tuple-element.250, f32[3,64,1024]{1,0,2:T(4,128)} %get-tuple-element.285, s32[]{:T(128)S(6)} %select_n.93, f32[64,128]{0,1:T(8,128)S(1)} %get-tuple-element.251, ...), kind=kOutput, calls=%fused_computation.34.clone.1 | convolution fusion | flops 38871040 | bytes 630788 | tf_op jit(solution)/shard_map/while/body/eval_jaxpr/pbc,kpb->kbc/dot_general | solution.py:166
  234.8 1.9 collective-permute-start.3
  236.7 2.5 copy.50
  239.3 4.0 %collective-permute-done.2 = bf16[1,3,1,128,128]{4,3,2,1,0:T(8,128)(2,1)} collective-permute-done((bf16[1,3,1,128,128]{4,3,2,1,0:T(8,128)(2,1)}, bf16[1,3,1,128,128]{4,3,2,1,0:T(8,128)(2,1)}, u32[]{:S(2)}, u32[]{:S(2)}) %collective-permute-start.2) | collective-permute-done | bytes 98336 | tf_op jit(solution)/shard_map/ppermute | solution.py:30
  243.3 1.3 maximum_convert_fusion
  244.6 2.2 fusion.42
  247.4 1.0 broadcast_select_fusion
  248.4 1.7 collective-permute-done.5
  250.1 4.1 %collective-permute-done.4 = f32[1,3,1,128,128]{4,3,2,1,0:T(8,128)S(1)} collective-permute-done((f32[1,3,1,128,128]{4,3,2,1,0:T(8,128)S(1)}, f32[1,3,1,128,128]{4,3,2,1,0:T(8,128)S(1)}, u32[]{:S(2)}, u32[]{:S(2)}) %collective-permute-start.4) | collective-permute-done | bytes 196640 | tf_op jit(solution)/shard_map/ppermute | solution.py:30
  254.2 2.1 fusion.50
  256.3 23.5 %all-reduce.4.cloned.1.call-done = f32[10240,128]{1,0:T(8,128)} async-done(((f32[10240,128]{1,0:T(8,128)}), f32[10240,128]{1,0:T(8,128)}) %all-reduce.4.cloned.1.call-update) | async-done | bytes 5242896 | tf_op jit(solution)/shard_map/psum | solution.py:226
  279.8 2.0 divide_subtract_fusion
  (117 shorter events, 34.2 us)
Async XLA Ops:
  7.2 14.4 %copy-start = (bf16[44,16,256]{2,1,0:T(8,128)(2,1)S(1)}, bf16[44,16,256]{2,1,0:T(8,128)(2,1)}, u32[]{:S(2)}) copy-start(bf16[44,16,256]{2,1,0:T(8,128)(2,1)} %param.21) | copy-start | bytes 1081348
  7.2 52.0 %all-gather.2.cloned.1.call-start = ((), (), s32[]{:S(2)}) async-start(), calls=%async_computation.2 | async-start | bytes 2785280 | tf_op jit(solution)/shard_map/all_gather | solution.py:208
  10.5 20.3 %all-to-all-start.1 = ((s32[128,1,1]{2,1,0:T(1,128)}), s32[128,1,1]{2,1,0:T(1,128)S(1)}, u32[]{:S(2)}, u32[]{:S(2)}) async-start(s32[128,1,1]{2,1,0:T(1,128)} %copy.48), calls=%async_computation.1 | async-start | bytes 131072 | tf_op jit(solution)/shard_map/all_to_all | solution.py:206
  22.2 14.4 %copy-start.3 = (f32[1,3,8,128,128]{4,3,2,1,0:T(8,128)S(1)}, f32[1,3,8,128,128]{4,3,2,1,0:T(8,128)}, u32[]{:S(2)}) copy-start(f32[1,3,8,128,128]{4,3,2,1,0:T(8,128)} %param.15) | copy-start | bytes 4718596
  30.7 9.5 %copy-start.12 = (s32[128,1,1]{2,1,0:T(1,128)}, s32[128,1,1]{2,1,0:T(1,128)S(1)}, u32[]{:S(2)}) copy-start(s32[128,1,1]{2,1,0:T(1,128)S(1)} %all-to-all-done.1) | copy-start | bytes 1540
  30.7 27.3 %all-to-all-start = ((bf16[128,16,256]{2,1,0:T(8,128)(2,1)}), bf16[128,16,256]{2,1,0:T(8,128)(2,1)}, u32[]{:S(2)}, u32[]{:S(2)}) async-start(bf16[128,16,256]{2,1,0:T(8,128)(2,1)} %copy.47), calls=%async_computation | async-start | bytes 2097152 | tf_op jit(solution)/shard_map/all_to_all | solution.py:205
  36.5 243.3 %all-reduce.4.cloned.1.call-start = ((), (), s32[]{:S(2)}) async-start(), calls=%async_computation.3 | async-start | bytes 10485760 | tf_op jit(solution)/shard_map/psum | solution.py:226
  37.3 11.6 %collective-permute-start.1 = (f32[1,3,1,128,128]{4,3,2,1,0:T(8,128)}, f32[1,3,1,128,128]{4,3,2,1,0:T(8,128)S(1)}, u32[]{:S(2)}, u32[]{:S(2)}) collective-permute-start(f32[1,3,1,128,128]{4,3,2,1,0:T(8,128)} %get-tuple-element.178), channel_id=1, source_target_pairs={{1,0},{2,1},{3,2},{4,3},{5,4},{6,5},{7,6},{8,7},{9,8},{10,9},{11,1... | collective-permute-start | bytes 589832 | tf_op jit(solution)/shard_map/ppermute | solution.py:32
  40.2 11.5 %collective-permute-start = (f32[1,3,1,128,128]{4,3,2,1,0:T(8,128)}, f32[1,3,1,128,128]{4,3,2,1,0:T(8,128)}, u32[]{:S(2)}, u32[]{:S(2)}) collective-permute-start(f32[1,3,1,128,128]{4,3,2,1,0:T(8,128)} %get-tuple-element.177), channel_id=1, source_target_pairs={{0,1},{1,2},{2,3},{3,4},{4,5},{5,6},{6,7},{7,8},{8,9},{9,10},{10,1... | collective-permute-start | bytes 589832 | tf_op jit(solution)/shard_map/ppermute | solution.py:30
  46.9 12.3 %copy-start.13 = (s32[128,1,1]{2,1,0:T(1,128)S(1)}, s32[128,1,1]{2,1,0:T(1,128)}, u32[]{:S(2)}) copy-start(s32[128,1,1]{2,1,0:T(1,128)} %copy-done.12) | copy-start | bytes 1540
  48.9 10.3 %copy-start.10 = (f32[1,3,1,128,128]{4,3,2,1,0:T(8,128)}, f32[1,3,1,128,128]{4,3,2,1,0:T(8,128)S(1)}, u32[]{:S(2)}) copy-start(f32[1,3,1,128,128]{4,3,2,1,0:T(8,128)S(1)} %collective-permute-done.1) | copy-start | bytes 589828
  69.1 2.4 copy-start.8
  71.6 8.6 %copy-start.2 = (f32[2048,1024]{1,0:T(8,128)}, f32[2048,1024]{1,0:T(8,128)S(1)}, u32[]{:S(2)}) copy-start(f32[2048,1024]{1,0:T(8,128)S(1)} %fusion.9) | copy-start | bytes 25165828 | tf_op jit(solution)/shard_map/cond
  81.9 3.8 %copy-start.4 = (bf16[2048,1024]{1,0:T(8,128)(2,1)S(1)}, bf16[2048,1024]{1,0:T(8,128)(2,1)}, u32[]{:S(2)}) copy-start(bf16[2048,1024]{1,0:T(8,128)(2,1)} %get-tuple-element.170) | copy-start | bytes 12582916 | tf_op jit(solution)/shard_map/cond
  81.9 6.2 %copy-start.16 = (f32[2048,1024]{1,0:T(8,128)S(1)}, f32[2048,1024]{1,0:T(8,128)}, u32[]{:S(2)}) copy-start(f32[2048,1024]{1,0:T(8,128)} %get-tuple-element.171) | copy-start | bytes 25165828 | tf_op jit(solution)/shard_map/cond
  85.7 7.3 %slice-start = ((s8[8388608]{0:T(1024)(128)(4,1)}), s8[4194304]{0:T(1024)(128)(4,1)S(1)}, s32[]{:S(2)}) async-start(s8[8388608]{0:T(1024)(128)(4,1)} %bitcast.65), calls=%async_computation.4 | async-start | bytes 8388608 | tf_op jit(solution)/shard_map/cond
  88.1 4.9 %slice-start.1 = ((s8[8388608]{0:T(1024)(128)(4,1)}), s8[4194304]{0:T(1024)(128)(4,1)S(1)}, s32[]{:S(2)}) async-start(s8[8388608]{0:T(1024)(128)(4,1)} %bitcast.65), calls=%async_computation.5 | async-start | bytes 8388608 | tf_op jit(solution)/shard_map/cond
  93.0 4.7 %copy-start.17 = (bf16[2048,1024]{1,0:T(8,128)(2,1)}, bf16[2048,1024]{1,0:T(8,128)(2,1)S(1)}, u32[]{:S(2)}) copy-start(bf16[2048,1024]{1,0:T(8,128)(2,1)S(1)} %multiply_convert_fusion.1) | copy-start | bytes 12582916 | tf_op jit(solution)/shard_map/cond
  233.2 0.9 copy-start.5
  234.8 4.5 %collective-permute-start.3 = (bf16[1,3,1,128,128]{4,3,2,1,0:T(8,128)(2,1)}, bf16[1,3,1,128,128]{4,3,2,1,0:T(8,128)(2,1)S(1)}, u32[]{:S(2)}, u32[]{:S(2)}) collective-permute-start(bf16[1,3,1,128,128]{4,3,2,1,0:T(8,128)(2,1)} %get-tuple-element.180), channel_id=1, source_target_pairs={{1,0},{2,1},{3,2},{4,3},{5,4},{6,5},{7,6},{8,7},{9,8},{10,9},{11,1... | collective-permute-start | bytes 294920 | tf_op jit(solution)/shard_map/ppermute | solution.py:32
  236.7 6.6 %collective-permute-start.2 = (bf16[1,3,1,128,128]{4,3,2,1,0:T(8,128)(2,1)}, bf16[1,3,1,128,128]{4,3,2,1,0:T(8,128)(2,1)}, u32[]{:S(2)}, u32[]{:S(2)}) collective-permute-start(bf16[1,3,1,128,128]{4,3,2,1,0:T(8,128)(2,1)} %get-tuple-element.179), channel_id=1, source_target_pairs={{0,1},{1,2},{2,3},{3,4},{4,5},{5,6},{6,7},{7,8},{8,9},{9,10},{10,1... | collective-permute-start | bytes 294920 | tf_op jit(solution)/shard_map/ppermute | solution.py:30
  239.2 5.4 %copy-start.11 = (f32[1,3,1,128,128]{4,3,2,1,0:T(8,128)S(1)}, f32[1,3,1,128,128]{4,3,2,1,0:T(8,128)}, u32[]{:S(2)}) copy-start(f32[1,3,1,128,128]{4,3,2,1,0:T(8,128)} %copy-done.10) | copy-start | bytes 589828
  244.6 2.8 copy-start.6
  244.6 2.8 copy-start.7
  246.9 3.3 %collective-permute-start.5 = (f32[1,3,1,128,128]{4,3,2,1,0:T(8,128)S(1)}, f32[1,3,1,128,128]{4,3,2,1,0:T(8,128)S(1)}, u32[]{:S(2)}, u32[]{:S(2)}) collective-permute-start(f32[1,3,1,128,128]{4,3,2,1,0:T(8,128)S(1)} %get-tuple-element.176), channel_id=1, source_target_pairs={{1,0},{2,1},{3,2},{4,3},{5,4},{6,5},{7,6},{8,7},{9,8},{10,9},{11,1... | collective-permute-start | bytes 589832 | tf_op jit(solution)/shard_map/ppermute | solution.py:32
  246.9 7.3 %collective-permute-start.4 = (f32[1,3,1,128,128]{4,3,2,1,0:T(8,128)S(1)}, f32[1,3,1,128,128]{4,3,2,1,0:T(8,128)S(1)}, u32[]{:S(2)}, u32[]{:S(2)}) collective-permute-start(f32[1,3,1,128,128]{4,3,2,1,0:T(8,128)S(1)} %get-tuple-element.175), channel_id=1, source_target_pairs={{0,1},{1,2},{2,3},{3,4},{4,5},{5,6},{6,7},{7,8},{8,9},{9,10},{10,1... | collective-permute-start | bytes 589832 | tf_op jit(solution)/shard_map/ppermute | solution.py:30
  248.4 31.4 %copy-start.9 = (f32[640,128]{1,0:T(8,128)S(1)}, f32[640,128]{1,0:T(8,128)}, u32[]{:S(2)}) copy-start(f32[640,128]{1,0:T(8,128)} %param.23) | copy-start | bytes 983044
  248.4 31.4 %copy-start.14 = (f32[640,128]{1,0:T(8,128)S(1)}, f32[640,128]{1,0:T(8,128)}, u32[]{:S(2)}) copy-start(f32[640,128]{1,0:T(8,128)} %param.24) | copy-start | bytes 983044
  248.4 31.4 %copy-start.15 = (f32[640,128]{1,0:T(8,128)S(1)}, f32[640,128]{1,0:T(8,128)}, u32[]{:S(2)}) copy-start(f32[640,128]{1,0:T(8,128)} %param.25) | copy-start | bytes 983044
  254.2 27.6 %copy-start.1 = (bf16[44,16,256]{2,1,0:T(8,128)(2,1)S(1)}, bf16[44,16,256]{2,1,0:T(8,128)(2,1)}, u32[]{:S(2)}) copy-start(bf16[44,16,256]{2,1,0:T(8,128)(2,1)} %param.21) | copy-start | bytes 1081348
Sparse Core Ops, SparseCore 0:
  10.3 48.8 all-gather.1
  122.7 157.0 all-reduce.3
where the time goes:
time: 292 us; the launch traced here: 289 us
  matrix products  113 us (39%)
  local copies, waits for them, and re-layouts  58 us (20%)
  waiting for transfers between devices  48.3 us (17%)
  other arithmetic  26.8 us (9%)
  starting transfers between devices  22.4 us (8%)
  between operations  14.2 us (5%)
  loops' own time  6.45 us (2%)
    dot_general x8, matrix products, block_group(): jnp.einsum('pbc,kbc->kpb', onehot, gas_part, precision=lax.Precision.HIGH...  44 us
    dot_general x8, matrix products, block_group(): jnp.einsum('pbc,kpb->kbc', onehot, handed, precision=lax.Precision.HIGHEST)  27.6 us
    psum x1, waiting for transfers between devices, shards(): complete = lax.psum(gradient, ('grp', 'dev'))  23.5 us
    dot_general x3, matrix products, contract_rows(): lax.dot_general(left_side, right_side, (((0,), (0,)), ((), ())), preferre...  20.7 us
    all_to_all x1, starting transfers between devices, shards(): lax.all_to_all(live_flags, ('grp', 'dev'), split_axis=0, concat_axis=0, t...  11.1 us
    ppermute x3, waiting for transfers between devices, extended_2(): lax.ppermute(tail, axis, [(i, (i + 1) % count) for i in range(count)])  10.9 us
    unnamed x30, local copies, waits for them, and re-layouts  9.55 us
    dot_general x1, matrix products, model_grads(): jnp.dot(act_first, w_second, preferred_element_type=jnp.float32)  8.56 us
  transfers between devices with their start and end apart: 10, of which 9 were waited for; matrix products, arithmetic and copies ran while one was open for 45% of the time, Pallas kernels for 0%

commit v1 on v0

v1 whole, which is shorter than its diff:
```python
import functools

import jax
import jax.numpy as jnp
from jax import lax
from jax.experimental import pallas as pl
from jax.experimental.pallas import tpu as pltpu
from jax.sharding import PartitionSpec as P

MESH = pl.DeviceIdType.MESH
F32 = jnp.float32
BF16 = jnp.bfloat16

KAPPA = 0.15
BETA_ONE = 0.9
BETA_TWO = 0.95
ADAM_EPS = 1e-08
LEARN_RATE = 0.001
ADAM_STEP = 10

BLK = 44
ROWS = 704
PIECE = 80
PARTS = (("x", 0, 24), ("y", 24, 32), ("z", 56, 24))
VMEM_LIMIT = 56 * 1024 * 1024


def coords():
    g = lax.axis_index("grp")
    d = lax.axis_index("dev")
    z = (g // 4) * 2 + (d // 2) % 2
    return d // 4, g % 4, z, d % 2


def device(x, y, z, core):
    return ((z // 2) * 4 + y, x * 4 + (z % 2) * 2 + core)


def on_axis(axis, x, y, z, k):
    return (
        (x + k) % 4 if axis == "x" else x,
        (y + k) % 4 if axis == "y" else y,
        (z + k) % 4 if axis == "z" else z,
    )


def evolves():
    g = lax.axis_index("grp")
    return jnp.logical_not((g == 0) | (g == 4) | (g == 2))


class Copies:
    def __init__(self, send_sem, recv_sem):
        self.send_sem, self.recv_sem = send_sem, recv_sem
        self.count = 0

    def make(self, src, dst, where):
        n = self.count
        self.count += 1
        return pltpu.make_async_remote_copy(
            src_ref=src,
            dst_ref=dst,
            send_sem=self.send_sem.at[n],
            recv_sem=self.recv_sem.at[n],
            device_id=where,
            device_id_type=MESH,
        )

    def start(self, src, dst, where):
        copy = self.make(src, dst, where)
        copy.start()
        return copy


def greet(partners):
    barrier = pltpu.get_barrier_semaphore()
    for partner in partners:
        pl.semaphore_signal(barrier, inc=1, device_id=partner, device_id_type=MESH)
    pl.semaphore_wait(barrier, len(partners))


def slab_device(step):
    d = lax.axis_index("dev")
    return (lax.axis_index("grp"), (d + step + 16) % 16)


def axis_partners():
    x, y, z, core = coords()
    found = [device(x, y, z, 1 - core)]
    for axis in ("x", "y", "z"):
        for k in (1, 2, 3):
            found.append(device(*on_axis(axis, x, y, z, k), core))
    g, d = lax.axis_index("grp"), lax.axis_index("dev")
    found.append((g, (d + 15 + 2 * core) % 16))
    return found


def gather_kernel(
    w_ref, ids_ref, gas_ref, wall_ref, total_ref, halo_ref, cnt, cnt_in, send_sem, recv_sem
):
    x, y, z, core = coords()
    d = lax.axis_index("dev")
    sibling = device(x, y, z, 1 - core)
    for j in range(8):
        wall_ref[j, d] = w_ref[pl.ds(j, PIECE, stride=8), :].astype(BF16)
    lanes = lax.broadcasted_iota(jnp.int32, (BLK, 128), 1)
    mine = (ids_ref[...] == lanes).astype(F32)
    cnt[0] = jnp.broadcast_to(jnp.sum(mine, axis=0, keepdims=True), (8, 128))
    greet(axis_partners())
    net = Copies(send_sem, recv_sem)
    sent = []

    def shard(px, pz, pc):
        return wall_ref.at[:, px * 4 + (pz % 2) * 2 + pc]

    def give(px, pz, pc, where):
        copy = net.start(shard(px, pz, pc), shard(px, pz, pc), where)
        sent.append(copy)
        return copy

    zm = z + 1 - 2 * (z % 2)
    count_copy = net.start(cnt.at[0], cnt_in.at[0], sibling)
    sent.append(count_copy)
    from_z = give(x, z, core, device(x, y, zm, core))
    own_x = [give(x, z, core, device((x + k) % 4, y, z, core)) for k in (1, 2, 3)]
    own_d2d = give(x, z, core, sibling)
    low = net.make(gas_ref.at[:, pl.ds(6, 2)], halo_ref.at[:, pl.ds(0, 2)], slab_device(1))
    high = net.make(gas_ref.at[:, pl.ds(0, 2)], halo_ref.at[:, pl.ds(2, 2)], slab_device(-1))

    @pl.when(evolves())
    def _():
        low.start()
        high.start()

    from_z.wait_recv()
    far_x = [give(x, zm, core, device((x + k) % 4, y, z, core)) for k in (1, 2, 3)]
    d2d = [own_d2d, give(x, zm, core, sibling)]
    count_copy.wait_recv()
    cnt[1] = cnt[0] + cnt_in[0]
    at, slot = 1, 1
    for axis in ("x", "y", "z"):
        copies = []
        for k in (1, 2, 3):
            copies.append(
                net.start(cnt.at[at], cnt_in.at[slot], device(*on_axis(axis, x, y, z, k), core))
            )
            slot += 1
        sent.extend(copies)
        for copy in copies:
            copy.wait_recv()
        cnt[at + 1] = cnt[at] + cnt_in[slot - 3] + cnt_in[slot - 2] + cnt_in[slot - 1]
        at += 1
    total_ref[...] = cnt[at]
    for k, copy in zip((1, 2, 3), own_x):
        copy.wait_recv()
        d2d.append(give((x + 4 - k) % 4, z, core, sibling))
    for k, copy in zip((1, 2, 3), far_x):
        copy.wait_recv()
        d2d.append(give((x + 4 - k) % 4, zm, core, sibling))
    for copy in d2d:
        copy.wait_recv()
    for copy in sent:
        copy.wait_send()

    @pl.when(evolves())
    def _():
        low.wait()
        high.wait()


def gas_first_kernel(
    gas_ref, halo_ref, pv_ref, cell_ref, fill_ref, rate_ref, mass_ref,
    pout_ref, dep_ref, sm, cpair, hs, ob,
):
    @pl.when(jnp.logical_not(evolves()))
    def _():
        pout_ref[...] = pv_ref[...]

    @pl.when(evolves())
    def _():
        for k in range(3):
            for i in range(8):
                lower = halo_ref[k, 1] if i == 0 else gas_ref[k, i - 1]
                upper = halo_ref[k, 2] if i == 7 else gas_ref[k, i + 1]
                sm[k, pl.ds(i * 128, 128), :] = 0.5 * gas_ref[k, i] + 0.25 * (lower + upper)
        lane = lax.broadcasted_iota(jnp.int32, (128, 128), 1)
        slots = lax.broadcasted_iota(jnp.int32, (64, 128), 0)
        left_lanes = lane < 64

        def tile(t, carry):
            l0 = pl.multiple_of(t * 128, 128)
            r0 = pl.multiple_of(t * 128 + 512, 128)
            cols = (pl.ds(l0, 128), pl.ds(r0, 128))
            index = jnp.concatenate([cell_ref[:, c] for c in cols], axis=0).T
            cpair[cols[0], :] = index
            for k in range(3):
                found = [
                    jnp.take_along_axis(sm[k, c, :], index, axis=1, mode="promise_in_bounds")
                    for c in cols
                ]
                gas_at = jnp.where(left_lanes, found[0], found[1]).T
                hands = []
                for side, c in enumerate(cols):
                    velocity, rate = pv_ref[k, :, c], rate_ref[:, c]
                    live = slots < fill_ref[:, c]
                    relaxed = (velocity + rate * gas_at[64 * side : 64 * side + 64]) / (1.0 + rate)
                    pout_ref[k, :, c] = jnp.where(live, relaxed, velocity)
                    hands.append(jnp.where(live, mass_ref[:, c] * (velocity - relaxed), 0.0))
                handed = jnp.concatenate(hands, axis=0).T
                coarse = handed.astype(BF16).astype(F32)
                fine = handed - coarse
                base = t * 2048
                for first, part in ((0, coarse), (8, fine)):
                    hs[pl.ds(base + first + k, 128, stride=16), :] = jnp.where(left_lanes, part, 0.0)
                    hs[pl.ds(base + first + 3 + k, 128, stride=16), :] = jnp.where(
                        left_lanes, 0.0, part
                    )
            zero = jnp.zeros((128, 128), F32)
            for row in (6, 7, 14, 15):
                hs[pl.ds(t * 2048 + row, 128, stride=16), :] = zero
            return carry

        lax.fori_loop(0, 4, tile, 0)
        cells = lax.broadcasted_iota(jnp.int32, (128, 128), 0)
        upper_rows = lax.broadcasted_iota(jnp.int32, (32, 128), 0) < 16

        def deposit(step, carry):
            for u in range(4):
                b = step * 4 + u
                values = hs[pl.ds(pl.multiple_of(b * 32, 32), 32), :]
                left = jnp.concatenate(
                    [jnp.where(upper_rows, values, 0.0), jnp.where(upper_rows, 0.0, values)], axis=1
                ).astype(BF16)
                hot = jnp.concatenate(
                    [
                        (cells == cpair[pl.ds(2 * b + i, 1), :]).astype(F32).astype(BF16)
                        for i in range(2)
                    ],
                    axis=1,
                )
                out = lax.dot_general(
                    left, hot, (((1,), (1,)), ((), ())), preferred_element_type=F32
                )
                ob[pl.ds(pl.multiple_of(b * 16, 16), 16), :] = jnp.concatenate(
                    [out[0:8] + out[8:16], out[16:24] + out[24:32]], axis=0
                )
            return carry

        lax.fori_loop(0, 64, deposit, 0)
        for k in range(3):
            for side in range(2):
                dep_ref[k, pl.ds(512 * side, 512), :] = ob[
                    pl.ds(3 * side + k, 512, stride=8), :
                ]


def dot(left, right, dims=((1,), (0,))):
    return lax.dot_general(left, right, (dims, ((), ())), preferred_element_type=F32)


def train_kernel(
    xy_ref, ids_ref, total_ref, wall_ref, grad_ref,
    a1, s1, a2, s2, b2, b1, err, w3f, w3, scale,
):
    for j in range(8):
        w3f[pl.ds(j, 128, stride=8), :] = wall_ref[j, pl.ds(1152, 128), :].astype(F32)
    for i in range(4):
        w3[i] = w3f[pl.ds(256 * i, 256), :].astype(BF16)
    lanes = lax.broadcasted_iota(jnp.int32, (BLK, 128), 1)
    inverse = 1.0 / jnp.maximum(total_ref[0:1, :], 1.0)
    picked = jnp.where(ids_ref[...] == lanes, inverse, 0.0)
    per_block = jnp.broadcast_to(jnp.sum(picked, axis=1, keepdims=True), (BLK, 128))
    for n in range(BLK):
        scale[pl.ds(16 * n, 16), :] = jnp.broadcast_to(per_block[n : n + 1], (16, 128))

    def columns(j, first, rows):
        return jnp.concatenate(
            [wall_ref[2 * j + i, pl.ds(first, rows), :] for i in range(2)], axis=1
        )

    def activate(pre, act, slope, j):
        s = 1.0 / (1.0 + jnp.exp(-pre))
        value = pre * s
        act[j] = value.astype(BF16)
        slope[j] = s * (1.0 + pre * (1.0 - s))

    def first(j, c):
        activate(dot(xy_ref[:, 0:128], columns(j, 0, 128)), a1, s1, j)
        return c

    lax.fori_loop(0, 4, first, 0)

    def second(j, c):
        acts = jnp.concatenate([a1[i] for i in range(4)], axis=1)
        activate(dot(acts, columns(j, 128, 1024)), a2, s2, j)
        return c

    lax.fori_loop(0, 4, second, 0)
    acts = jnp.concatenate([a2[i] for i in range(4)], axis=1)
    predicted = dot(acts, jnp.concatenate([w3[i] for i in range(4)], axis=0))
    err[...] = ((predicted - xy_ref[:, 128:256].astype(F32)) * scale[...]).astype(BF16)

    def third_back(j, c):
        w3f[pl.ds(pl.multiple_of(j * 256, 256), 256), :] = dot(a2[j], err[...], ((0,), (0,)))
        b2[j] = (dot(err[...], w3[j], ((1,), (1,))) * s2[j]).astype(BF16)
        return c

    lax.fori_loop(0, 4, third_back, 0)
    for j in range(8):
        grad_ref[j, pl.ds(1152, 128), :] = w3f[pl.ds(j, 128, stride=8), :]

    def second_back(i, c):
        h0 = pl.multiple_of(128 + i * 256, 128)
        for j in range(4):
            piece = dot(a1[i], b2[j], ((0,), (0,)))
            grad_ref[2 * j, pl.ds(h0, 256), :] = piece[:, :128]
            grad_ref[2 * j + 1, pl.ds(h0, 256), :] = piece[:, 128:]
        backs = jnp.concatenate([b2[j] for j in range(4)], axis=1)
        rows = jnp.concatenate([wall_ref[j, pl.ds(h0, 256), :] for j in range(8)], axis=1)
        b1[i] = (dot(backs, rows, ((1,), (1,))) * s1[i]).astype(BF16)
        return c

    lax.fori_loop(0, 4, second_back, 0)

    def first_back(j, c):
        piece = dot(xy_ref[:, 0:128], b1[j], ((0,), (0,)))
        grad_ref[2 * j, pl.ds(0, 128), :] = piece[:, :128]
        grad_ref[2 * j + 1, pl.ds(0, 128), :] = piece[:, 128:]
        return c

    lax.fori_loop(0, 4, first_back, 0)


def gas_second(gas_ref, halo_ref, dep_ref, dep_halo, gout_ref, mid):
    row = lax.broadcasted_iota(jnp.int32, (128, 128), 0)
    col = lax.broadcasted_iota(jnp.int32, (128, 128), 1)

    def walls(f):
        return (
            jnp.where(row == 0, 0.0, pltpu.roll(f, 1, 0))
            + jnp.where(row == 127, 0.0, pltpu.roll(f, 127, 0))
            + jnp.where(col == 0, 0.0, pltpu.roll(f, 1, 1))
            + jnp.where(col == 127, 0.0, pltpu.roll(f, 127, 1))
        )

    def component(k, c):
        def gas(i):
            if i < 0:
                return halo_ref[k, i + 2]
            return gas_ref[k, i] if i < 8 else halo_ref[k, i - 6]

        def dep(i):
            if i < 0:
                return dep_halo[0, k, i + 2].astype(F32)
            if i < 8:
                return dep_ref[k, pl.ds(i * 128, 128), :]
            return dep_halo[1, k, i - 8].astype(F32)

        for i in range(-1, 9):
            f = gas(i)
            step = f + KAPPA * (gas(i - 1) + gas(i + 1) + walls(f) - 6.0 * f)
            mid[i + 1] = step + 0.5 * dep(i) + 0.25 * (dep(i - 1) + dep(i + 1))
        for i in range(8):
            f = mid[i + 1]
            gout_ref[k, i] = f + KAPPA * (mid[i] + mid[i + 2] + walls(f) - 6.0 * f)
        return c

    lax.fori_loop(0, 3, component, 0)


def reduce_kernel(
    grad_ref, w_ref, m_ref, v_ref, gas_ref, halo_ref, dep_ref,
    wout_ref, mout_ref, vout_ref, gout_ref,
    sum_x, sum_y, sum_z, in1_x, in1_y, in1_z, in2_x, in2_y, in2_z, in3_x, in3_y, in3_z,
    fin, flat, dep_out, dep_halo, mid, send_sem, recv_sem,
):
    x, y, z, core = coords()
    zh, zl = z // 2, z % 2
    g = lax.axis_index("grp")
    d = lax.axis_index("dev")
    sibling = device(x, y, z, 1 - core)

    @pl.when(evolves())
    def _():
        for k in range(3):
            for i in range(2):
                dep_out[0, k, i] = dep_ref[k, pl.ds(128 * (6 + i), 128), :].astype(BF16)
                dep_out[1, k, i] = dep_ref[k, pl.ds(128 * i, 128), :].astype(BF16)

    partners = axis_partners()
    partners += [device(x, (y + k) % 4, (z + 2) % 4, core) for k in (1, 2, 3)]
    greet(partners)
    net = Copies(send_sem, recv_sem)
    sent = []
    sums = (sum_x, sum_y, sum_z)
    inputs = ((in1_x, in1_y, in1_z), (in2_x, in2_y, in2_z), (in3_x, in3_y, in3_z))
    order = (("x", "y", "z"), ("y", "z", "x"), ("z", "x", "y"))

    low = net.make(dep_out.at[0], dep_halo.at[0], slab_device(1))
    high = net.make(dep_out.at[1], dep_halo.at[1], slab_device(-1))

    @pl.when(evolves())
    def _():
        low.start()
        high.start()

    pair = []
    for part, (_, r0, n) in enumerate(PARTS):
        pair.append(
            net.start(
                grad_ref.at[:, :, :, :, 1 - core, pl.ds(r0, n)], sums[part].at[...], sibling
            )
        )
    sent += pair

    def view(ref, part, done, phase, k):
        axis = order[part][phase]
        nx, ny, nz = on_axis(axis, x, y, z, k)
        full = slice(None)
        index = [full, full, full, full]
        for a in done + (axis,):
            if a == "x":
                index[2] = nx
            elif a == "y":
                index[1] = ny
            else:
                index[0], index[3] = nz // 2, nz % 2
        return tuple(index)

    waiting = [None, None, None]

    def send(part, phase):
        done = order[part][:phase]
        waiting[part] = []
        for k in (1, 2, 3):
            nx, ny, nz = on_axis(order[part][phase], x, y, z, k)
            waiting[part].append(
                net.start(
                    sums[part].at[view(sums[part], part, done, phase, k)],
                    inputs[phase][part].at[k - 1],
                    device(nx, ny, nz, core),
                )
            )
        sent.extend(waiting[part])

    for part, (_, r0, n) in enumerate(PARTS):
        pair[part].wait_recv()
        sums[part][...] = sums[part][...] + grad_ref[:, :, :, :, core, pl.ds(r0, n), :]
        send(part, 0)

    @pl.when(evolves())
    def _():
        low.wait()
        high.wait()
        gas_second(gas_ref, halo_ref, dep_ref, dep_halo, gout_ref, mid)

    @pl.when(jnp.logical_not(evolves()))
    def _():
        gout_ref[...] = gas_ref[...]

    for phase in range(3):
        for part, (_, r0, n) in enumerate(PARTS):
            for copy in waiting[part]:
                copy.wait_recv()
            here = view(sums[part], part, order[part][:phase], phase, 0)
            come = inputs[phase][part]
            total = sums[part][here] + come[0] + come[1] + come[2]
            if phase < 2:
                sums[part][here] = total
                send(part, phase + 1)
            else:
                fin[g, pl.ds(r0, n), :] = total
    across = []
    for k in range(1, 8):
        across.append(net.start(fin.at[g], fin.at[g], ((g + k) % 8, d)))
    sent += across
    for copy in across:
        copy.wait_recv()
    for j in range(8):
        flat[pl.ds(j, PIECE, stride=8), :] = fin[j]
    gradient = flat[...]
    first_new = BETA_ONE * m_ref[...] + (1.0 - BETA_ONE) * gradient
    second_new = BETA_TWO * v_ref[...] + (1.0 - BETA_TWO) * gradient * gradient
    mout_ref[...] = first_new
    vout_ref[...] = second_new
    first_hat = first_new / (1.0 - BETA_ONE**ADAM_STEP)
    second_hat = second_new / (1.0 - BETA_TWO**ADAM_STEP)
    wout_ref[...] = w_ref[...] - LEARN_RATE * first_hat / (jnp.sqrt(second_hat) + ADAM_EPS)
    for copy in sent:
        copy.wait_send()


def in_vmem(count):
    return [pl.BlockSpec(memory_space=pltpu.VMEM)] * count


def shards(
    gas_velocity, parcel_velocity, parcel_cell, block_fill, relax_rate, parcel_mass,
    sample_blocks, learner_ids, master_weights, first_moment, second_moment,
):
    shape = jax.ShapeDtypeStruct
    ids = jnp.broadcast_to(learner_ids[:, None], (BLK, 128))
    gas = gas_velocity[0]
    wall, total, halo = pl.pallas_call(
        gather_kernel,
        name="weights_counts_halo",
        out_shape=(
            shape((8, 16, PIECE, 128), BF16),
            shape((8, 128), F32),
            shape((3, 4, 128, 128), F32),
        ),
        in_specs=in_vmem(3),
        out_specs=tuple(in_vmem(3)),
        scratch_shapes=[
            pltpu.VMEM((5, 8, 128), F32),
            pltpu.VMEM((10, 8, 128), F32),
            pltpu.SemaphoreType.DMA((32,)),
            pltpu.SemaphoreType.DMA((32,)),
        ],
        compiler_params=pltpu.CompilerParams(
            collective_id=0, has_side_effects=True, vmem_limit_bytes=VMEM_LIMIT
        ),
    )(master_weights, ids, gas)
    parcels, deposit = pl.pallas_call(
        gas_first_kernel,
        name="parcels",
        out_shape=(shape((3, 64, 1024), F32), shape((3, 1024, 128), F32)),
        in_specs=in_vmem(7),
        out_specs=tuple(in_vmem(2)),
        scratch_shapes=[
            pltpu.VMEM((3, 1024, 128), F32),
            pltpu.VMEM((512, 128), jnp.int32),
            pltpu.VMEM((8192, 128), F32),
            pltpu.VMEM((4096, 128), F32),
        ],
        compiler_params=pltpu.CompilerParams(vmem_limit_bytes=VMEM_LIMIT),
    )(gas, halo, parcel_velocity[0], parcel_cell[0], block_fill, relax_rate[0], parcel_mass[0])
    grads = pl.pallas_call(
        train_kernel,
        name="train",
        out_shape=shape((8, 1280, 128), F32),
        in_specs=in_vmem(4),
        out_specs=in_vmem(1)[0],
        scratch_shapes=[
            pltpu.VMEM((4, ROWS, 256), BF16),
            pltpu.VMEM((4, ROWS, 256), F32),
            pltpu.VMEM((4, ROWS, 256), BF16),
            pltpu.VMEM((4, ROWS, 256), F32),
            pltpu.VMEM((4, ROWS, 256), BF16),
            pltpu.VMEM((4, ROWS, 256), BF16),
            pltpu.VMEM((ROWS, 128), BF16),
            pltpu.VMEM((1024, 128), F32),
            pltpu.VMEM((4, 256, 128), BF16),
            pltpu.VMEM((ROWS, 128), F32),
        ],
        compiler_params=pltpu.CompilerParams(vmem_limit_bytes=VMEM_LIMIT),
    )(sample_blocks.reshape(ROWS, 256), ids, total, wall.reshape(8, 1280, 128))
    sizes = [n for _, _, n in PARTS]
    first_in = [
        pltpu.VMEM((3, 2, 4, 2, sizes[0], 128), F32),
        pltpu.VMEM((3, 2, 4, 2, sizes[1], 128), F32),
        pltpu.VMEM((3, 4, 4, sizes[2], 128), F32),
    ]
    second_in = [
        pltpu.VMEM((3, 2, 2, sizes[0], 128), F32),
        pltpu.VMEM((3, 4, sizes[1], 128), F32),
        pltpu.VMEM((3, 4, sizes[2], 128), F32),
    ]
    third_in = [pltpu.VMEM((3, n, 128), F32) for n in sizes]
    master_out, first_out, second_out, gas_out = pl.pallas_call(
        reduce_kernel,
        name="reduce_update_diffuse",
        out_shape=(
            shape((640, 128), F32),
            shape((640, 128), F32),
            shape((640, 128), F32),
            shape((3, 8, 128, 128), F32),
        ),
        in_specs=in_vmem(7),
        out_specs=tuple(in_vmem(4)),
        scratch_shapes=[pltpu.VMEM((2, 4, 4, 2, n, 128), F32) for n in sizes]
        + first_in
        + second_in
        + third_in
        + [
            pltpu.VMEM((8, PIECE, 128), F32),
            pltpu.VMEM((640, 128), F32),
            pltpu.VMEM((2, 3, 2, 128, 128), BF16),
            pltpu.VMEM((2, 3, 2, 128, 128), BF16),
            pltpu.VMEM((10, 128, 128), F32),
            pltpu.SemaphoreType.DMA((48,)),
            pltpu.SemaphoreType.DMA((48,)),
        ],
        compiler_params=pltpu.CompilerParams(
            collective_id=1, has_side_effects=True, vmem_limit_bytes=VMEM_LIMIT
        ),
    )(
        grads.reshape(2, 4, 4, 2, 2, PIECE, 128),
        master_weights, first_moment, second_moment, gas, halo, deposit,
    )
    return gas_out[None], parcels[None], master_out, first_out, second_out


def solution(mesh):
    placed = (
        P("grp", None, "dev", None, None),
        P("grp", None, None, "dev"),
        P("grp", None, "dev"),
        P("grp", "dev"),
        P("grp", None, "dev"),
        P("grp", None, "dev"),
        P(("grp", "dev"), None, None),
        P(("grp", "dev")),
        P("dev", None),
        P("dev", None),
        P("dev", None),
    )
    return jax.shard_map(
        shards,
        mesh=mesh,
        in_specs=placed,
        out_specs=(
            P("grp", None, "dev", None, None),
            P("grp", None, None, "dev"),
            P("dev", None),
            P("dev", None),
            P("dev", None),
        ),
        check_vma=False,
    )
```

time: 292 us -> 126 us (0.43); the launches traced: 289 us -> 126 us
  Pallas kernels: 0 us -> 119 us
  matrix products: 113 us -> 0 us
  local copies, waits for them, and re-layouts: 58 us -> 6.3 us
  waiting for transfers between devices: 48.3 us -> 0 us
  other arithmetic: 26.8 us -> 0 us
  starting transfers between devices: 22.4 us -> 0 us
  between operations: 14.2 us -> 0.68 us
  loops' own time: 6.45 us -> 0 us
    pallas_call x0 -> x4, Pallas kernels: none -> 119 us  [the longest x1 59.9 us: shards(): pl.pallas_call(reduce_kernel, name='reduce_update_diffuse', out_shape=(sh...]
    dot_general x24 -> x0, matrix products: 113 us -> none  [the longest x8 44 us: block_group(): jnp.einsum('pbc,kbc->kpb', onehot, gas_part, precision=lax.Precision.HIGH...]
    dynamic_slice x32 -> x0, local copies, waits for them, and re-layouts: 25.2 us -> none  [the longest x8 7.54 us: block_group(): gas_part = lax.dynamic_slice_in_dim(smoothed, block_start, group_size, 1)]
    psum x1 -> x0, waiting for transfers between devices: 23.5 us -> none  [shards(): complete = lax.psum(gradient, ('grp', 'dev'))]
    all_to_all x2 -> x0, starting transfers between devices: 16.9 us -> none  [the longest x1 11.1 us: shards(): lax.all_to_all(live_flags, ('grp', 'dev'), split_axis=0, concat_axis=0, t...]
    ppermute x6 -> x0, waiting for transfers between devices: 12.7 us -> none  [the longest x3 10.9 us: extended_2(): lax.ppermute(tail, axis, [(i, (i + 1) % count) for i in range(count)])]
    add x11 -> x0, other arithmetic: 12.3 us -> none  [the longest x8 7.16 us: block_group(): relaxed = (velocity_part + rate_part * gas_at) / (1.0 + rate_part)]
    all_to_all x2 -> x0, waiting for transfers between devices: 10.9 us -> none  [the longest x1 6.94 us: shards(): lax.all_to_all(live_flags, ('grp', 'dev'), split_axis=0, concat_axis=0, t...]
  transfers between devices with their start and end apart: 10 -> 0, of which waited for: 9 -> 0; matrix products, arithmetic and copies ran while one was open for 45% -> 0% of each run, Pallas kernels for 0% -> 0%
where the time goes in v1:
time: 126 us
  Pallas kernels  119 us (94%)
  local copies, waits for them, and re-layouts  6.3 us (5%)
    pallas_call x1, Pallas kernels, shards(): pl.pallas_call(reduce_kernel, name='reduce_update_diffuse', out_shape=(sh...  59.9 us
    pallas_call x1, Pallas kernels, shards(): pl.pallas_call(gather_kernel, name='weights_counts_halo', out_shape=(shap...  39.3 us
    pallas_call x1, Pallas kernels, shards(): pl.pallas_call(train_kernel, name='train', out_shape=shape((8, 1280, 128)...  16 us
    unnamed x10, local copies, waits for them, and re-layouts  4.97 us
    pallas_call x1, Pallas kernels, shards(): pl.pallas_call(gas_first_kernel, name='parcels', out_shape=(shape((3, 64,...  3.52 us

profile of v1, /device:TPU:0, one launch (start us, length us, event | category | flops | bytes accessed | tf_op | source)
XLA Modules:
  0.0 125.7 jit_solution(3803319133519478467)
XLA Ops:
  0.6 1.3 %broadcast_in_dim.12.ids_ref = s32[44,128]{1,0:T(8,128)} broadcast(s32[44]{0:T(128)} %param.18), dimensions={0} | broadcast | bytes 22704 | tf_op jit(solution)/shard_map/broadcast_in_dim | solution.py:502
  2.0 39.3 %weights_counts_halo.1 = (bf16[8,16,80,128]{3,2,1,0:T(8,128)(2,1)}, f32[8,128]{1,0:T(8,128)}, f32[3,4,128,128]{3,2,1,0:T(8,128)}) custom-call(f32[640,128]{1,0:T(8,128)} %w_ref.3, s32[44,128]{1,0:T(8,128)} %broadcast_in_dim.12.ids_ref, f32[3,8,128,128]{3,2,1,0:T(8,128)} %bitcast.11), custom_call_target="tpu_custom_call" | custom-call | tf_op jit(solution)/shard_map/weights_counts_halo/pallas_call | solution.py:504
  41.3 16.0 %train.1 = f32[8,1280,128]{2,1,0:T(8,128)} custom-call(bf16[704,256]{1,0:T(8,128)(2,1)} %bitcast.17, s32[44,128]{1,0:T(8,128)} %broadcast_in_dim.12.ids_ref, f32[8,128]{1,0:T(8,128)} %get-tuple-element.14.total_ref, bf16[8,1280,128]{2,1,0:T(8,128)(2,1)} %bitcast.14), custom_call_target="tpu_custom_call" | custom-call | tf_op jit(solution)/shard_map/train/pallas_call | solution.py:538
  57.2 3.5 %parcels.1 = (f32[3,64,1024]{2,1,0:T(8,128)}, f32[3,1024,128]{2,1,0:T(8,128)}) custom-call(f32[3,8,128,128]{3,2,1,0:T(8,128)} %bitcast.12, f32[3,4,128,128]{3,2,1,0:T(8,128)} %get-tuple-element.16.halo_ref, f32[3,64,1024]{2,1,0:T(8,128)} %bitcast.16, s32[64,1024]{1,0:T(8,128)} %bitcast.18, s32[1,1024]{1,0:T(1,128)} %fill_ref.1, f32[64,1024]{1,0:T(8,128)} %bitcast.19, ...), custom_call_target="tpu_custom_call" | custom-call | tf_op jit(solution)/shard_map/parcels/pallas_call | solution.py:524
  60.8 59.9 %reduce_update_diffuse.1 = (f32[640,128]{1,0:T(8,128)}, f32[640,128]{1,0:T(8,128)}, f32[640,128]{1,0:T(8,128)}, f32[3,8,128,128]{3,2,1,0:T(8,128)}) custom-call(f32[2,4,4,2,2,80,128]{6,5,4,3,2,1,0:T(8,128)} %bitcast.10, f32[640,128]{1,0:T(8,128)} %w_ref.3, f32[640,128]{1,0:T(8,128)} %m_ref.1, f32[640,128]{1,0:T(8,128)} %v_ref.1, ...), custom_call_target="tpu_custom_call" | custom-call | tf_op jit(solution)/shard_map/reduce_update_diffuse/pallas_call | solution.py:570
  120.7 0.0 copy-start.2
  120.7 0.0 copy-start.1
  120.7 0.0 copy-start
  120.7 2.8 %copy.20 = f32[1,3,8,128,128]{4,3,2,1,0:T(8,128)} copy(f32[1,3,8,128,128]{4,3,2,1,0:T(8,128)} %bitcast.15) | data formatting | bytes 3145728
  123.5 0.0 copy-done.2
  123.5 0.7 copy.21
  124.2 0.0 copy-done.1
  124.2 0.7 copy.22
  124.9 0.0 copy-done
  124.9 0.7 copy.23
Async XLA Ops:
  120.7 2.8 %copy-start.2 = (f32[640,128]{1,0:T(8,128)S(1)}, f32[640,128]{1,0:T(8,128)}, u32[]{:S(2)}) copy-start(f32[640,128]{1,0:T(8,128)} %get-tuple-element.30) | copy-start | bytes 983044
  120.7 3.5 %copy-start.1 = (f32[640,128]{1,0:T(8,128)S(1)}, f32[640,128]{1,0:T(8,128)}, u32[]{:S(2)}) copy-start(f32[640,128]{1,0:T(8,128)} %get-tuple-element.31) | copy-start | bytes 983044
  120.7 4.2 %copy-start = (f32[640,128]{1,0:T(8,128)S(1)}, f32[640,128]{1,0:T(8,128)}, u32[]{:S(2)}) copy-start(f32[640,128]{1,0:T(8,128)} %get-tuple-element.32) | copy-start | bytes 983044

commit v2 on v0

v2 whole, which is shorter than its diff:
```python
import functools

import jax
import jax.numpy as jnp
from jax import lax
from jax.experimental import pallas as pl
from jax.experimental.pallas import tpu as pltpu
from jax.sharding import PartitionSpec as P

MESH = pl.DeviceIdType.MESH
F32 = jnp.float32
BF16 = jnp.bfloat16

KAPPA = 0.15
BETA_ONE = 0.9
BETA_TWO = 0.95
ADAM_EPS = 1e-08
LEARN_RATE = 0.001
ADAM_STEP = 10

BLK = 44
ROWS = 704
PIECE = 80
PARTS = (("x", 0, 24), ("y", 24, 32), ("z", 56, 24))
VMEM_LIMIT = 60 * 1024 * 1024
RECV_X = 140


def coords():
    g = lax.axis_index("grp")
    d = lax.axis_index("dev")
    z = (g // 4) * 2 + (d // 2) % 2
    return d // 4, g % 4, z, d % 2


def device(x, y, z, core):
    return ((z // 2) * 4 + y, x * 4 + (z % 2) * 2 + core)


def on_axis(axis, x, y, z, k):
    return (
        (x + k) % 4 if axis == "x" else x,
        (y + k) % 4 if axis == "y" else y,
        (z + k) % 4 if axis == "z" else z,
    )


def evolves():
    g = lax.axis_index("grp")
    return jnp.logical_not((g == 0) | (g == 4) | (g == 2))


class Copies:
    def __init__(self, send_sem, recv_sem):
        self.send_sem, self.recv_sem = send_sem, recv_sem
        self.count = 0

    def make(self, src, dst, where):
        n = self.count
        self.count += 1
        return pltpu.make_async_remote_copy(
            src_ref=src,
            dst_ref=dst,
            send_sem=self.send_sem.at[n],
            recv_sem=self.recv_sem.at[n],
            device_id=where,
            device_id_type=MESH,
        )

    def start(self, src, dst, where):
        copy = self.make(src, dst, where)
        copy.start()
        return copy


def greet(partners):
    barrier = pltpu.get_barrier_semaphore()
    for partner in partners:
        pl.semaphore_signal(barrier, inc=1, device_id=partner, device_id_type=MESH)
    pl.semaphore_wait(barrier, len(partners))


def slab_device(step):
    d = lax.axis_index("dev")
    return (lax.axis_index("grp"), (d + step + 16) % 16)


def all_partners():
    x, y, z, core = coords()
    found = [device(x, y, z, 1 - core)]
    for axis in ("x", "y", "z"):
        for k in (1, 2, 3):
            found.append(device(*on_axis(axis, x, y, z, k), core))
    g, d = lax.axis_index("grp"), lax.axis_index("dev")
    found.append((g, (d + 15 + 2 * core) % 16))
    found += [device(x, (y + k) % 4, (z + 2) % 4, core) for k in (1, 2, 3)]
    return found


def dot(left, right, dims=((1,), (0,))):
    return lax.dot_general(left, right, (dims, ((), ())), preferred_element_type=F32)


def smooth(gas_ref, halo_ref, sm, layers):
    for k in range(3):
        for i in layers:
            lower = halo_ref[k, 1] if i == 0 else gas_ref[k, i - 1]
            upper = halo_ref[k, 2] if i == 7 else gas_ref[k, i + 1]
            sm[k, pl.ds(i * 128, 128), :] = 0.5 * gas_ref[k, i] + 0.25 * (lower + upper)


def drag(t, pv_ref, cell_ref, fill_ref, rate_ref, mass_ref, pout_ref, sm, cpair, hs):
    lane = lax.broadcasted_iota(jnp.int32, (128, 128), 1)
    slots = lax.broadcasted_iota(jnp.int32, (64, 128), 0)
    left_lanes = lane < 64
    cols = (pl.ds(t * 128, 128), pl.ds(t * 128 + 512, 128))
    index = jnp.concatenate([cell_ref[:, c] for c in cols], axis=0).T
    cpair[cols[0], :] = index
    for k in range(3):
        found = [
            jnp.take_along_axis(sm[k, c, :], index, axis=1, mode="promise_in_bounds") for c in cols
        ]
        gas_at = jnp.where(left_lanes, found[0], found[1]).T
        hands = []
        for side, c in enumerate(cols):
            velocity, rate = pv_ref[k, :, c], rate_ref[:, c]
            live = slots < fill_ref[:, c]
            relaxed = (velocity + rate * gas_at[64 * side : 64 * side + 64]) / (1.0 + rate)
            pout_ref[k, :, c] = jnp.where(live, relaxed, velocity)
            hands.append(jnp.where(live, mass_ref[:, c] * (velocity - relaxed), 0.0))
        handed = jnp.concatenate(hands, axis=0).T
        coarse = handed.astype(BF16).astype(F32)
        fine = handed - coarse
        base = t * 2048
        for first, part in ((0, coarse), (8, fine)):
            hs[pl.ds(base + first + k, 128, stride=16), :] = jnp.where(left_lanes, part, 0.0)
            hs[pl.ds(base + first + 3 + k, 128, stride=16), :] = jnp.where(left_lanes, 0.0, part)
    zero = jnp.zeros((128, 128), F32)
    for row in (6, 7, 14, 15):
        hs[pl.ds(t * 2048 + row, 128, stride=16), :] = zero


def deposit(t, cpair, hs, ob, dep):
    cells = lax.broadcasted_iota(jnp.int32, (128, 128), 0)
    upper_rows = lax.broadcasted_iota(jnp.int32, (32, 128), 0) < 16

    def several(step, carry):
        for u in range(8):
            b = t * 64 + step * 8 + u
            values = hs[pl.ds(pl.multiple_of(b * 32, 32), 32), :]
            left = jnp.concatenate(
                [jnp.where(upper_rows, values, 0.0), jnp.where(upper_rows, 0.0, values)], axis=1
            ).astype(BF16)
            hot = jnp.concatenate(
                [
                    (cells == cpair[pl.ds(2 * b + i, 1), :]).astype(F32).astype(BF16)
                    for i in range(2)
                ],
                axis=1,
            )
            out = dot(left, hot, ((1,), (1,)))
            ob[pl.ds(pl.multiple_of(b * 16, 16), 16), :] = jnp.concatenate(
                [out[0:8] + out[8:16], out[16:24] + out[24:32]], axis=0
            )
        return carry

    lax.fori_loop(0, 8, several, 0)
    for k in range(3):
        for side in range(2):
            dep[k, pl.ds(512 * side + 128 * t, 128), :] = ob[
                pl.ds(1024 * t + 3 * side + k, 128, stride=8), :
            ]


def gas_second(gas_ref, halo_ref, dep_ref, dep_halo, gout_ref, mid):
    row = lax.broadcasted_iota(jnp.int32, (128, 128), 0)
    col = lax.broadcasted_iota(jnp.int32, (128, 128), 1)

    def walls(f):
        return (
            jnp.where(row == 0, 0.0, pltpu.roll(f, 1, 0))
            + jnp.where(row == 127, 0.0, pltpu.roll(f, 127, 0))
            + jnp.where(col == 0, 0.0, pltpu.roll(f, 1, 1))
            + jnp.where(col == 127, 0.0, pltpu.roll(f, 127, 1))
        )

    def component(k, c):
        def gas(i):
            if i < 0:
                return halo_ref[k, i + 2]
            return gas_ref[k, i] if i < 8 else halo_ref[k, i - 6]

        def dep(i):
            if i < 0:
                return dep_halo[0, k, i + 2].astype(F32)
            if i < 8:
                return dep_ref[k, pl.ds(i * 128, 128), :]
            return dep_halo[1, k, i - 8].astype(F32)

        for i in range(-1, 9):
            f = gas(i)
            step = f + KAPPA * (gas(i - 1) + gas(i + 1) + walls(f) - 6.0 * f)
            mid[i + 1] = step + 0.5 * dep(i) + 0.25 * (dep(i - 1) + dep(i + 1))
        for i in range(8):
            f = mid[i + 1]
            gout_ref[k, i] = f + KAPPA * (mid[i] + mid[i + 2] + walls(f) - 6.0 * f)
        return c

    lax.fori_loop(0, 3, component, 0)


def step_kernel(
    w_ref, m_ref, v_ref, ids_ref, xy_ref, gas_ref, pv_ref, cell_ref, fill_ref, rate_ref, mass_ref,
    wout_ref, mout_ref, vout_ref, gout_ref, pout_ref,
    wall, halo, cnt, cnt_in, sm, cpair, hs, ob, dep, dep_out, dep_halo, mid,
    a1, s1, a2, s2, b2, b1, err, w3f, w3, scale,
    grad, pair_sum, in1_x, in1_y, in1_z, sum1_x, sum1_y, sum1_z, in2_x, in2_y, in2_z,
    sum2_x, sum2_y, sum2_z, in3_x, in3_y, in3_z, fin, flat, send_sem, recv_sem,
):
    x, y, z, core = coords()
    zh, zl = z // 2, z % 2
    g, d = lax.axis_index("grp"), lax.axis_index("dev")
    sibling = device(x, y, z, 1 - core)
    evo = evolves()
    net = Copies(send_sem, recv_sem)
    sent = []

    def push(src, dst, where):
        copy = net.start(src, dst, where)
        sent.append(copy)
        return copy

    def when_evolving(*steps):
        @pl.when(evo)
        def _():
            for step in steps:
                step()

    for j in range(8):
        wall[j, pl.ds(pl.multiple_of(d * PIECE, 16), PIECE), :] = w_ref[
            pl.ds(j, PIECE, stride=8), :
        ].astype(BF16)
    lanes = lax.broadcasted_iota(jnp.int32, (BLK, 128), 1)
    mine = (ids_ref[...] == lanes).astype(F32)
    cnt[0] = jnp.broadcast_to(jnp.sum(mine, axis=0, keepdims=True), (8, 128))
    greet(all_partners())

    def shard(px, pz, pc, j0, jn):
        first = pl.multiple_of((px * 4 + (pz % 2) * 2 + pc) * PIECE, 16)
        return wall.at[pl.ds(j0, jn), pl.ds(first, PIECE)]

    def give(px, pz, j0, jn, where):
        piece = shard(px, pz, core, j0, jn)
        return push(piece, piece, where)

    half = (y % 2) * 4
    zm = z + 1 - 2 * zl
    from_z = [
        give(x, z, 0, 4, device(x, y, (z + 1) % 4, core)),
        give(x, z, 4, 4, device(x, y, (z + 3) % 4, core)),
    ]
    near_x = [give(x, z, half, 4, device((x + k) % 4, y, z, core)) for k in (1, 2, 3)]
    over = [give(x, z, 0, 8, sibling)]
    count_copy = push(cnt.at[0], cnt_in.at[0], sibling)
    low = net.make(gas_ref.at[:, pl.ds(6, 2)], halo.at[:, pl.ds(0, 2)], slab_device(1))
    high = net.make(gas_ref.at[:, pl.ds(0, 2)], halo.at[:, pl.ds(2, 2)], slab_device(-1))

    def parcels(t):
        drag(t, pv_ref, cell_ref, fill_ref, rate_ref, mass_ref, pout_ref, sm, cpair, hs)

    when_evolving(
        low.start,
        high.start,
        lambda: smooth(gas_ref, halo, sm, range(1, 7)),
        lambda: parcels(1),
        lambda: parcels(2),
    )
    for copy in from_z:
        copy.wait_recv()
    far_x = [give(x, zm, half, 4, device((x + k) % 4, y, z, core)) for k in (1, 2, 3)]
    over.append(give(x, zm, 0, 8, sibling))
    when_evolving(lambda: deposit(1, cpair, hs, ob, dep))

    up, down = device(x, (y + 1) % 4, z, core), device(x, (y + 3) % 4, z, core)
    from_y = []
    for pz, copies in ((z, near_x), (zm, far_x)):
        for k, copy in zip((1, 2, 3), copies):
            copy.wait_recv()
            px = (x + 4 - k) % 4
            from_y.append((px, pz, 0, give(px, pz, half, 2, up)))
            from_y.append((px, pz, 2, give(px, pz, half + 2, 2, down)))
            over.append(give(px, pz, half, 4, sibling))
        if pz is z:
            when_evolving(lambda: deposit(2, cpair, hs, ob, dep))
    other = 4 - half
    for px, pz, q, copy in from_y:
        copy.wait_recv()
        over.append(give(px, pz, other + q, 2, sibling))
    count_copy.wait_recv()
    cnt[1] = cnt[0] + cnt_in[0]

    def count_send(axis, at, slot):
        return [
            push(cnt.at[at], cnt_in.at[slot + k], device(*on_axis(axis, x, y, z, k + 1), core))
            for k in range(3)
        ]

    def count_add(copies, at, slot):
        for copy in copies:
            copy.wait_recv()
        cnt[at + 1] = cnt[at] + cnt_in[slot] + cnt_in[slot + 1] + cnt_in[slot + 2]

    counting = count_send("x", 1, 1)
    for copy in over:
        copy.wait_recv()

    for j in range(8):
        w3f[pl.ds(j, 128, stride=8), :] = wall[j, pl.ds(1152, 128), :].astype(F32)
    for i in range(4):
        w3[i] = w3f[pl.ds(256 * i, 256), :].astype(BF16)

    def columns(j, first, rows):
        return jnp.concatenate([wall[2 * j + i, pl.ds(first, rows), :] for i in range(2)], axis=1)

    def activate(pre, act, slope, j):
        s = 0.5 * jnp.tanh(0.5 * pre) + 0.5
        value = pre * s
        act[j] = value.astype(BF16)
        slope[j] = s + value * (1.0 - s)

    def first(j, c):
        activate(dot(xy_ref[:, 0:128], columns(j, 0, 128)), a1, s1, j)
        return c

    def second(j, c):
        acts = jnp.concatenate([a1[i] for i in range(4)], axis=1)
        activate(dot(acts, columns(j, 128, 1024)), a2, s2, j)
        return c

    lax.fori_loop(0, 4, first, 0)
    count_add(counting, 1, 1)
    counting = count_send("y", 2, 4)
    lax.fori_loop(0, 2, second, 0)
    count_add(counting, 2, 4)
    counting = count_send("z", 3, 7)
    lax.fori_loop(2, 4, second, 0)
    count_add(counting, 3, 7)
    inverse = 1.0 / jnp.maximum(cnt[4, 0:1, :], 1.0)
    picked = jnp.where(ids_ref[...] == lanes, inverse, 0.0)
    per_block = jnp.broadcast_to(jnp.sum(picked, axis=1, keepdims=True), (BLK, 128))
    for n in range(BLK):
        scale[pl.ds(16 * n, 16), :] = jnp.broadcast_to(per_block[n : n + 1], (16, 128))
    acts = jnp.concatenate([a2[i] for i in range(4)], axis=1)
    predicted = dot(acts, jnp.concatenate([w3[i] for i in range(4)], axis=0))
    err[...] = ((predicted - xy_ref[:, 128:256].astype(F32)) * scale[...]).astype(BF16)

    def third_back(j, c):
        w3f[pl.ds(pl.multiple_of(j * 256, 256), 256), :] = dot(a2[j], err[...], ((0,), (0,)))
        b2[j] = (dot(err[...], w3[j], ((1,), (1,))) * s2[j]).astype(BF16)
        return c

    lax.fori_loop(0, 4, third_back, 0)
    for j in range(8):
        grad[j // 4, j % 4, pl.ds(1152, 128), :] = w3f[pl.ds(j, 128, stride=8), :]

    def grad_second(i):
        for j in range(4):
            piece = dot(a1[i], b2[j], ((0,), (0,)))
            for e in range(2):
                n = 2 * j + e
                grad[n // 4, n % 4, pl.ds(128 + 256 * i, 256), :] = piece[:, 128 * e : 128 * e + 128]

    def back_first(i, c):
        h0 = pl.multiple_of(128 + i * 256, 128)
        backs = jnp.concatenate([b2[j] for j in range(4)], axis=1)
        rows = jnp.concatenate([wall[j, pl.ds(h0, 256), :] for j in range(8)], axis=1)
        b1[i] = (dot(backs, rows, ((1,), (1,))) * s1[i]).astype(BF16)
        return c

    (_, x0, xn), (_, y0, yn), (_, z0, zn) = PARTS
    pairs = {}

    def pair_start(px):
        pairs[px] = [
            push(
                grad.at[:, :, pl.ds(pl.multiple_of((px * 4 + q * 2 + 1 - core) * PIECE, 8), PIECE)],
                pair_sum.at[px, q],
                sibling,
            )
            for q in range(2)
        ]

    first_x = {}
    first_y, first_z = [], []

    def pair_done(px):
        for q, copy in enumerate(pairs[px]):
            copy.wait_recv()
            own = pl.ds(pl.multiple_of((px * 4 + q * 2 + core) * PIECE, 8), PIECE)
            pair_sum[px, q] = pair_sum[px, q] + grad[:, :, own, :]
        k = (px - x + 4) % 4
        slot = jnp.maximum(k - 1, 0)
        n = net.count
        net.count += 1
        copy = pltpu.make_async_remote_copy(
            src_ref=pair_sum.at[px, :, :, :, pl.ds(x0, xn)],
            dst_ref=in1_x.at[slot],
            send_sem=send_sem.at[n],
            recv_sem=recv_x.at[slot],
            device_id=device(px, y, z, core),
            device_id_type=MESH,
        )
        first_x[px] = copy

        @pl.when(k > 0)
        def _():
            copy.start()

        for k in (1, 2, 3):
            ny = (y + k) % 4
            first_y.append(
                push(
                    pair_sum.at[px, :, :, ny, pl.ds(y0, yn)],
                    in1_y.at[k - 1, px],
                    device(x, ny, z, core),
                )
            )
        for k in (1, 2, 3):
            nz = (z + k) % 4
            first_z.append(
                push(
                    pair_sum.at[px, nz % 2, nz // 2, :, pl.ds(z0, zn)],
                    in1_z.at[k - 1, px],
                    device(x, y, nz, core),
                )
            )

    recv_x = recv_sem.at[pl.ds(RECV_X, 3)]
    grad_second(3)
    pair_start(3)
    grad_second(2)
    pair_start(2)
    pair_done(3)
    grad_second(1)
    pair_done(2)
    grad_second(0)
    pair_start(1)
    lax.fori_loop(0, 4, back_first, 0)
    pair_done(1)
    for j in range(4):
        piece = dot(xy_ref[:, 0:128], b1[j], ((0,), (0,)))
        for e in range(2):
            n = 2 * j + e
            grad[n // 4, n % 4, pl.ds(0, 128), :] = piece[:, 128 * e : 128 * e + 128]
    pair_start(0)
    pair_done(0)

    def send_deposit():
        for k in range(3):
            for i in range(2):
                dep_out[0, k, i] = dep[k, pl.ds(128 * (6 + i), 128), :].astype(BF16)
                dep_out[1, k, i] = dep[k, pl.ds(128 * i, 128), :].astype(BF16)
        dep_low.start()
        dep_high.start()

    dep_low = net.make(dep_out.at[0], dep_halo.at[0], slab_device(1))
    dep_high = net.make(dep_out.at[1], dep_halo.at[1], slab_device(-1))
    when_evolving(
        low.wait,
        high.wait,
        lambda: smooth(gas_ref, halo, sm, (0, 7)),
        lambda: parcels(0),
        lambda: parcels(3),
        lambda: deposit(0, cpair, hs, ob, dep),
        lambda: deposit(3, cpair, hs, ob, dep),
        send_deposit,
    )

    for k in (1, 2, 3):
        pltpu.make_async_remote_copy(
            src_ref=in1_x.at[k - 1],
            dst_ref=in1_x.at[k - 1],
            send_sem=send_sem.at[0],
            recv_sem=recv_x.at[k - 1],
            device_id=sibling,
            device_id_type=MESH,
        ).wait_recv()
    sum1_x[...] = pair_sum[x, :, :, :, pl.ds(x0, xn), :] + in1_x[0] + in1_x[1] + in1_x[2]
    second_x = [
        push(sum1_x.at[:, :, (y + k) % 4], in2_x.at[k - 1], device(x, (y + k) % 4, z, core))
        for k in (1, 2, 3)
    ]
    for copy in first_z:
        copy.wait_recv()
    sum1_z[...] = pair_sum[:, zl, zh, :, pl.ds(z0, zn), :] + in1_z[0] + in1_z[1] + in1_z[2]
    second_z = [
        push(sum1_z.at[(x + k) % 4], in2_z.at[k - 1], device((x + k) % 4, y, z, core))
        for k in (1, 2, 3)
    ]
    for copy in first_y:
        copy.wait_recv()
    sum1_y[...] = pair_sum[:, :, :, y, pl.ds(y0, yn), :] + in1_y[0] + in1_y[1] + in1_y[2]
    second_y = []
    for k in (1, 2, 3):
        nz = (z + k) % 4
        second_y.append(
            push(sum1_y.at[:, nz % 2, nz // 2], in2_y.at[k - 1], device(x, y, nz, core))
        )
    for copy in second_x:
        copy.wait_recv()
    sum2_x[...] = sum1_x[:, :, y] + in2_x[0] + in2_x[1] + in2_x[2]
    third_x = []
    for k in (1, 2, 3):
        nz = (z + k) % 4
        third_x.append(push(sum2_x.at[nz % 2, nz // 2], in3_x.at[k - 1], device(x, y, nz, core)))
    for copy in second_z:
        copy.wait_recv()
    sum2_z[...] = sum1_z[x] + in2_z[0] + in2_z[1] + in2_z[2]
    third_z = [
        push(sum2_z.at[(y + k) % 4], in3_z.at[k - 1], device(x, (y + k) % 4, z, core))
        for k in (1, 2, 3)
    ]
    for copy in second_y:
        copy.wait_recv()
    sum2_y[...] = sum1_y[:, zl, zh] + in2_y[0] + in2_y[1] + in2_y[2]
    third_y = [
        push(sum2_y.at[(x + k) % 4], in3_y.at[k - 1], device((x + k) % 4, y, z, core))
        for k in (1, 2, 3)
    ]
    for copy in third_x + third_z + third_y:
        copy.wait_recv()
    fin[g, pl.ds(x0, xn), :] = sum2_x[zl, zh] + in3_x[0] + in3_x[1] + in3_x[2]
    fin[g, pl.ds(y0, yn), :] = sum2_y[x] + in3_y[0] + in3_y[1] + in3_y[2]
    fin[g, pl.ds(z0, zn), :] = sum2_z[y] + in3_z[0] + in3_z[1] + in3_z[2]
    across = [push(fin.at[g], fin.at[g], ((g + k) % 8, d)) for k in range(1, 8)]

    when_evolving(
        dep_low.wait,
        dep_high.wait,
        lambda: gas_second(gas_ref, halo, dep, dep_halo, gout_ref, mid),
    )

    @pl.when(jnp.logical_not(evo))
    def _():
        gout_ref[...] = gas_ref[...]
        pout_ref[...] = pv_ref[...]

    for copy in across:
        copy.wait_recv()
    for j in range(8):
        flat[pl.ds(j, PIECE, stride=8), :] = fin[j]
    gradient = flat[...]
    first_new = BETA_ONE * m_ref[...] + (1.0 - BETA_ONE) * gradient
    second_new = BETA_TWO * v_ref[...] + (1.0 - BETA_TWO) * gradient * gradient
    mout_ref[...] = first_new
    vout_ref[...] = second_new
    first_hat = first_new / (1.0 - BETA_ONE**ADAM_STEP)
    second_hat = second_new / (1.0 - BETA_TWO**ADAM_STEP)
    wout_ref[...] = w_ref[...] - LEARN_RATE * first_hat / (jnp.sqrt(second_hat) + ADAM_EPS)
    for copy in sent:
        copy.wait_send()
    for px in range(4):

        @pl.when(px != x)
        def _():
            first_x[px].wait_send()


def in_vmem(count):
    return [pl.BlockSpec(memory_space=pltpu.VMEM)] * count


def shards(
    gas_velocity, parcel_velocity, parcel_cell, block_fill, relax_rate, parcel_mass,
    sample_blocks, learner_ids, master_weights, first_moment, second_moment,
):
    shape = jax.ShapeDtypeStruct
    ids = jnp.broadcast_to(learner_ids[:, None], (BLK, 128))
    (_, _, xn), (_, _, yn), (_, _, zn) = PARTS

    def buf(*dims, dtype=F32):
        return pltpu.VMEM(dims, dtype)

    scratch = [
        buf(8, 1280, 128, dtype=BF16),
        buf(3, 4, 128, 128),
        buf(5, 8, 128),
        buf(10, 8, 128),
        buf(3, 1024, 128),
        buf(512, 128, dtype=jnp.int32),
        buf(8192, 128),
        buf(4096, 128),
        buf(3, 1024, 128),
        buf(2, 3, 2, 128, 128, dtype=BF16),
        buf(2, 3, 2, 128, 128, dtype=BF16),
        buf(10, 128, 128),
        buf(4, ROWS, 256, dtype=BF16),
        buf(4, ROWS, 256),
        buf(4, ROWS, 256, dtype=BF16),
        buf(4, ROWS, 256),
        buf(4, ROWS, 256, dtype=BF16),
        buf(4, ROWS, 256, dtype=BF16),
        buf(ROWS, 128, dtype=BF16),
        buf(1024, 128),
        buf(4, 256, 128, dtype=BF16),
        buf(ROWS, 128),
        buf(2, 4, 1280, 128),
        buf(4, 2, 2, 4, PIECE, 128),
        buf(3, 2, 2, 4, xn, 128),
        buf(3, 4, 2, 2, yn, 128),
        buf(3, 4, 4, zn, 128),
        buf(2, 2, 4, xn, 128),
        buf(4, 2, 2, yn, 128),
        buf(4, 4, zn, 128),
        buf(3, 2, 2, xn, 128),
        buf(3, 4, yn, 128),
        buf(3, 4, zn, 128),
        buf(2, 2, xn, 128),
        buf(4, yn, 128),
        buf(4, zn, 128),
        buf(3, xn, 128),
        buf(3, yn, 128),
        buf(3, zn, 128),
        buf(8, PIECE, 128),
        buf(640, 128),
        pltpu.SemaphoreType.DMA((RECV_X,)),
        pltpu.SemaphoreType.DMA((RECV_X + 3,)),
    ]
    master_out, first_out, second_out, gas_out, parcels = pl.pallas_call(
        step_kernel,
        name="step",
        out_shape=(
            shape((640, 128), F32),
            shape((640, 128), F32),
            shape((640, 128), F32),
            shape((3, 8, 128, 128), F32),
            shape((3, 64, 1024), F32),
        ),
        in_specs=in_vmem(11),
        out_specs=tuple(in_vmem(5)),
        scratch_shapes=scratch,
        compiler_params=pltpu.CompilerParams(
            collective_id=0, has_side_effects=True, vmem_limit_bytes=VMEM_LIMIT
        ),
    )(
        master_weights, first_moment, second_moment, ids, sample_blocks.reshape(ROWS, 256),
        gas_velocity[0], parcel_velocity[0], parcel_cell[0], block_fill, relax_rate[0],
        parcel_mass[0],
    )
    return gas_out[None], parcels[None], master_out, first_out, second_out


def solution(mesh):
    placed = (
        P("grp", None, "dev", None, None),
        P("grp", None, None, "dev"),
        P("grp", None, "dev"),
        P("grp", "dev"),
        P("grp", None, "dev"),
        P("grp", None, "dev"),
        P(("grp", "dev"), None, None),
        P(("grp", "dev")),
        P("dev", None),
        P("dev", None),
        P("dev", None),
    )
    return jax.shard_map(
        shards,
        mesh=mesh,
        in_specs=placed,
        out_specs=(
            P("grp", None, "dev", None, None),
            P("grp", None, None, "dev"),
            P("dev", None),
            P("dev", None),
            P("dev", None),
        ),
        check_vma=False,
    )
```

time: 292 us -> 85.8 us (0.29); the launches traced: 289 us -> 85.7 us
  matrix products: 113 us -> 0 us
  Pallas kernels: 0 us -> 77.6 us
  local copies, waits for them, and re-layouts: 58 us -> 7.42 us
  waiting for transfers between devices: 48.3 us -> 0 us
  other arithmetic: 26.8 us -> 0 us
  starting transfers between devices: 22.4 us -> 0 us
  between operations: 14.2 us -> 0.66 us
  loops' own time: 6.45 us -> 0 us
    dot_general x24 -> x0, matrix products: 113 us -> none  [the longest x8 44 us: block_group(): jnp.einsum('pbc,kbc->kpb', onehot, gas_part, precision=lax.Precision.HIGH...]
    pallas_call x0 -> x1, Pallas kernels: none -> 77.6 us  [shards(): pl.pallas_call(step_kernel, name='step', out_shape=(shape((640, 128), F32...]
    dynamic_slice x32 -> x0, local copies, waits for them, and re-layouts: 25.2 us -> none  [the longest x8 7.54 us: block_group(): gas_part = lax.dynamic_slice_in_dim(smoothed, block_start, group_size, 1)]
    psum x1 -> x0, waiting for transfers between devices: 23.5 us -> none  [shards(): complete = lax.psum(gradient, ('grp', 'dev'))]
    all_to_all x2 -> x0, starting transfers between devices: 16.9 us -> none  [the longest x1 11.1 us: shards(): lax.all_to_all(live_flags, ('grp', 'dev'), split_axis=0, concat_axis=0, t...]
    ppermute x6 -> x0, waiting for transfers between devices: 12.7 us -> none  [the longest x3 10.9 us: extended_2(): lax.ppermute(tail, axis, [(i, (i + 1) % count) for i in range(count)])]
    add x11 -> x0, other arithmetic: 12.3 us -> none  [the longest x8 7.16 us: block_group(): relaxed = (velocity_part + rate_part * gas_at) / (1.0 + rate_part)]
    all_to_all x2 -> x0, waiting for transfers between devices: 10.9 us -> none  [the longest x1 6.94 us: shards(): lax.all_to_all(live_flags, ('grp', 'dev'), split_axis=0, concat_axis=0, t...]
  transfers between devices with their start and end apart: 10 -> 0, of which waited for: 9 -> 0; matrix products, arithmetic and copies ran while one was open for 45% -> 0% of each run, Pallas kernels for 0% -> 0%
where the time goes in v2:
time: 85.8 us; the launch traced here: 85.7 us
  Pallas kernels  77.6 us (90%)
  local copies, waits for them, and re-layouts  7.42 us (9%)
    pallas_call x1, Pallas kernels, shards(): pl.pallas_call(step_kernel, name='step', out_shape=(shape((640, 128), F32...  77.6 us
    unnamed x13, local copies, waits for them, and re-layouts  6.09 us

profile of v2, /device:TPU:0, one launch (start us, length us, event | category | flops | bytes accessed | tf_op | source)
XLA Modules:
  0.0 85.7 jit_solution(5412289908089031968)
XLA Ops:
  0.6 1.3 %broadcast_in_dim.12.ids_ref = s32[44,128]{1,0:T(8,128)} broadcast(s32[44]{0:T(128)} %param.18), dimensions={0} | broadcast | bytes 22704 | tf_op jit(solution)/shard_map/broadcast_in_dim | solution.py:578
  2.0 77.6 %step.1 = (f32[640,128]{1,0:T(8,128)}, f32[640,128]{1,0:T(8,128)}, f32[640,128]{1,0:T(8,128)}, f32[3,8,128,128]{3,2,1,0:T(8,128)}, f32[3,64,1024]{2,1,0:T(8,128)}) custom-call(f32[640,128]{1,0:T(8,128)} %w_ref.1, f32[640,128]{1,0:T(8,128)} %m_ref.1, f32[640,128]{1,0:T(8,128)} %v_ref.1, s32[44,128]{1,0:T(8,128)} %broadcast_in_dim.12.ids_ref, ...), custom_call_target="tpu_custom_call" | custom-call | tf_op jit(solution)/shard_map/step/pallas_call | solution.py:629
  79.6 0.0 copy-start
  79.6 2.8 %copy.21 = f32[1,3,8,128,128]{4,3,2,1,0:T(8,128)} copy(f32[1,3,8,128,128]{4,3,2,1,0:T(8,128)} %bitcast.9) | data formatting | bytes 3145728
  82.3 0.0 copy-done
  82.3 0.0 copy-start.3
  82.3 0.0 copy-start.2
  82.3 0.0 copy-start.1
  82.4 0.9 %copy.22 = f32[1,3,64,1024]{3,2,1,0:T(8,128)} copy(f32[1,3,64,1024]{3,2,1,0:T(8,128)S(1)} %bitcast.11) | data formatting | bytes 1572864
  83.2 0.2 copy-done.3
  83.5 0.7 copy.23
  84.2 0.0 copy-done.2
  84.2 0.7 copy.24
  84.9 0.0 copy-done.1
  84.9 0.7 copy.25
Async XLA Ops:
  79.6 2.8 %copy-start = (f32[3,64,1024]{2,1,0:T(8,128)S(1)}, f32[3,64,1024]{2,1,0:T(8,128)}, u32[]{:S(2)}) copy-start(f32[3,64,1024]{2,1,0:T(8,128)} %get-tuple-element.11) | copy-start | bytes 2359300
  82.3 1.1 %copy-start.3 = (f32[640,128]{1,0:T(8,128)S(1)}, f32[640,128]{1,0:T(8,128)}, u32[]{:S(2)}) copy-start(f32[640,128]{1,0:T(8,128)} %get-tuple-element.22) | copy-start | bytes 983044
  82.3 1.9 %copy-start.2 = (f32[640,128]{1,0:T(8,128)S(1)}, f32[640,128]{1,0:T(8,128)}, u32[]{:S(2)}) copy-start(f32[640,128]{1,0:T(8,128)} %get-tuple-element.23) | copy-start | bytes 983044
  82.3 2.6 %copy-start.1 = (f32[640,128]{1,0:T(8,128)S(1)}, f32[640,128]{1,0:T(8,128)}, u32[]{:S(2)}) copy-start(f32[640,128]{1,0:T(8,128)} %get-tuple-element.24) | copy-start | bytes 983044

commit v3 on v2

--- a/solution.py
+++ b/solution.py
@@ -1,5 +1,3 @@
-import functools
-
 import jax
 import jax.numpy as jnp
 from jax import lax
@@ -23,7 +21,7 @@
 PIECE = 80
 PARTS = (("x", 0, 24), ("y", 24, 32), ("z", 56, 24))
 VMEM_LIMIT = 60 * 1024 * 1024
-RECV_X = 140
+RECV_X = 150
 
 
 def coords():
@@ -71,13 +69,6 @@
         copy = self.make(src, dst, where)
         copy.start()
         return copy
-
-
-def greet(partners):
-    barrier = pltpu.get_barrier_semaphore()
-    for partner in partners:
-        pl.semaphore_signal(barrier, inc=1, device_id=partner, device_id_type=MESH)
-    pl.semaphore_wait(barrier, len(partners))
 
 
 def slab_device(step):
@@ -145,8 +136,8 @@
     upper_rows = lax.broadcasted_iota(jnp.int32, (32, 128), 0) < 16
 
     def several(step, carry):
-        for u in range(8):
-            b = t * 64 + step * 8 + u
+        for u in range(32):
+            b = t * 64 + step * 32 + u
             values = hs[pl.ds(pl.multiple_of(b * 32, 32), 32), :]
             left = jnp.concatenate(
                 [jnp.where(upper_rows, values, 0.0), jnp.where(upper_rows, 0.0, values)], axis=1
@@ -164,7 +155,7 @@
             )
         return carry
 
-    lax.fori_loop(0, 8, several, 0)
+    lax.fori_loop(0, 2, several, 0)
     for k in range(3):
         for side in range(2):
             dep[k, pl.ds(512 * side + 128 * t, 128), :] = ob[
@@ -210,8 +201,10 @@
 
 
 def step_kernel(
-    w_ref, m_ref, v_ref, ids_ref, xy_ref, gas_ref, pv_ref, cell_ref, fill_ref, rate_ref, mass_ref,
-    wout_ref, mout_ref, vout_ref, gout_ref, pout_ref,
+    ids_ref, w_in, xy_in, gas_in, pv_in, cell_in, fill_in, rate_in, mass_in,
+    grad_out, gas_out, parcel_out,
+    ids, w_ref, xy_ref, gas_ref, pv_ref, cell_ref, fill_ref, rate_ref, mass_ref, gout_ref, pout_ref,
+    in_sem, out_sem,
     wall, halo, cnt, cnt_in, sm, cpair, hs, ob, dep, dep_out, dep_halo, mid,
     a1, s1, a2, s2, b2, b1, err, w3f, w3, scale,
     grad, pair_sum, in1_x, in1_y, in1_z, sum1_x, sum1_y, sum1_z, in2_x, in2_y, in2_z,
@@ -236,14 +229,35 @@
             for step in steps:
                 step()
 
+    partners = all_partners()
+    barrier = pltpu.get_barrier_semaphore()
+    for partner in partners:
+        pl.semaphore_signal(barrier, inc=1, device_id=partner, device_id_type=MESH)
+    pairs_in = (
+        (w_in, w_ref), (gas_in, gas_ref), (cell_in, cell_ref), (pv_in, pv_ref), (rate_in, rate_ref),
+        (mass_in, mass_ref), (fill_in, fill_ref), (xy_in, xy_ref),
+    )
+    loads = [
+        pltpu.make_async_copy(src, dst, in_sem.at[i]) for i, (src, dst) in enumerate(pairs_in)
+    ]
+    for load in loads:
+        load.start()
+    for n in range(BLK):
+        ids[pl.ds(n, 1), :] = jnp.full((1, 128), ids_ref[n], jnp.int32)
+    gas_store = pltpu.make_async_copy(gout_ref, gas_out, out_sem.at[0])
+    parcel_store = pltpu.make_async_copy(pout_ref, parcel_out, out_sem.at[1])
+    gas_same = pltpu.make_async_copy(gas_ref, gas_out, out_sem.at[0])
+    parcel_same = pltpu.make_async_copy(pv_ref, parcel_out, out_sem.at[1])
+
+    loads[0].wait()
     for j in range(8):
         wall[j, pl.ds(pl.multiple_of(d * PIECE, 16), PIECE), :] = w_ref[
             pl.ds(j, PIECE, stride=8), :
         ].astype(BF16)
     lanes = lax.broadcasted_iota(jnp.int32, (BLK, 128), 1)
-    mine = (ids_ref[...] == lanes).astype(F32)
+    mine = (ids[...] == lanes).astype(F32)
     cnt[0] = jnp.broadcast_to(jnp.sum(mine, axis=0, keepdims=True), (8, 128))
-    greet(all_partners())
+    pl.semaphore_wait(barrier, len(partners))
 
     def shard(px, pz, pc, j0, jn):
         first = pl.multiple_of((px * 4 + (pz % 2) * 2 + pc) * PIECE, 16)
@@ -255,26 +269,47 @@
 
     half = (y % 2) * 4
     zm = z + 1 - 2 * zl
+    count_copy = push(cnt.at[0], cnt_in.at[0], sibling)
     from_z = [
         give(x, z, 0, 4, device(x, y, (z + 1) % 4, core)),
         give(x, z, 4, 4, device(x, y, (z + 3) % 4, core)),
     ]
     near_x = [give(x, z, half, 4, device((x + k) % 4, y, z, core)) for k in (1, 2, 3)]
     over = [give(x, z, 0, 8, sibling)]
-    count_copy = push(cnt.at[0], cnt_in.at[0], sibling)
     low = net.make(gas_ref.at[:, pl.ds(6, 2)], halo.at[:, pl.ds(0, 2)], slab_device(1))
     high = net.make(gas_ref.at[:, pl.ds(0, 2)], halo.at[:, pl.ds(2, 2)], slab_device(-1))
 
     def parcels(t):
         drag(t, pv_ref, cell_ref, fill_ref, rate_ref, mass_ref, pout_ref, sm, cpair, hs)
 
+    for load in loads[1:]:
+        load.wait()
+
+    @pl.when(jnp.logical_not(evo))
+    def _():
+        gas_same.start()
+        parcel_same.start()
+
     when_evolving(
-        low.start,
-        high.start,
         lambda: smooth(gas_ref, halo, sm, range(1, 7)),
         lambda: parcels(1),
         lambda: parcels(2),
     )
+    count_copy.wait_recv()
+    cnt[1] = cnt[0] + cnt_in[0]
+
+    def count_send(axis, at, slot):
+        return [
+            push(cnt.at[at], cnt_in.at[slot + k], device(*on_axis(axis, x, y, z, k + 1), core))
+            for k in range(3)
+        ]
+
+    def count_add(copies, at, slot):
+        for copy in copies:
+            copy.wait_recv()
+        cnt[at + 1] = cnt[at] + cnt_in[slot] + cnt_in[slot + 1] + cnt_in[slot + 2]
+
+    counting = count_send("y", 1, 1)
     for copy in from_z:
         copy.wait_recv()
     far_x = [give(x, zm, half, 4, device((x + k) % 4, y, z, core)) for k in (1, 2, 3)]
@@ -291,28 +326,19 @@
             from_y.append((px, pz, 2, give(px, pz, half + 2, 2, down)))
             over.append(give(px, pz, half, 4, sibling))
         if pz is z:
+            count_add(counting, 1, 1)
+            counting = count_send("z", 2, 4)
             when_evolving(lambda: deposit(2, cpair, hs, ob, dep))
+    count_add(counting, 2, 4)
+    counting = count_send("x", 3, 7)
     other = 4 - half
     for px, pz, q, copy in from_y:
         copy.wait_recv()
         over.append(give(px, pz, other + q, 2, sibling))
-    count_copy.wait_recv()
-    cnt[1] = cnt[0] + cnt_in[0]
-
-    def count_send(axis, at, slot):
-        return [
-            push(cnt.at[at], cnt_in.at[slot + k], device(*on_axis(axis, x, y, z, k + 1), core))
-            for k in range(3)
-        ]
-
-    def count_add(copies, at, slot):
-        for copy in copies:
-            copy.wait_recv()
-        cnt[at + 1] = cnt[at] + cnt_in[slot] + cnt_in[slot + 1] + cnt_in[slot + 2]
-
-    counting = count_send("x", 1, 1)
     for copy in over:
         copy.wait_recv()
+
+    when_evolving(low.start, high.start)
 
     for j in range(8):
         w3f[pl.ds(j, 128, stride=8), :] = wall[j, pl.ds(1152, 128), :].astype(F32)
@@ -338,15 +364,10 @@
         return c
 
     lax.fori_loop(0, 4, first, 0)
-    count_add(counting, 1, 1)
-    counting = count_send("y", 2, 4)
-    lax.fori_loop(0, 2, second, 0)
-    count_add(counting, 2, 4)
-    counting = count_send("z", 3, 7)
-    lax.fori_loop(2, 4, second, 0)
+    lax.fori_loop(0, 4, second, 0)
     count_add(counting, 3, 7)
     inverse = 1.0 / jnp.maximum(cnt[4, 0:1, :], 1.0)
-    picked = jnp.where(ids_ref[...] == lanes, inverse, 0.0)
+    picked = jnp.where(ids[...] == lanes, inverse, 0.0)
     per_block = jnp.broadcast_to(jnp.sum(picked, axis=1, keepdims=True), (BLK, 128))
     for n in range(BLK):
         scale[pl.ds(16 * n, 16), :] = jnp.broadcast_to(per_block[n : n + 1], (16, 128))
@@ -391,34 +412,49 @@
         ]
 
     first_x = {}
-    first_y, first_z = [], []
+    first_y, first_z = {}, {}
+
+    def to_x(px, src, slots, sems):
+        k = (px - x + 4) % 4
+        slot = jnp.maximum(k - 1, 0)
+        n = net.count
+        net.count += 1
+        copy = pltpu.make_async_remote_copy(
+            src_ref=src,
+            dst_ref=slots.at[slot],
+            send_sem=send_sem.at[n],
+            recv_sem=sems.at[slot],
+            device_id=device(px, y, z, core),
+            device_id_type=MESH,
+        )
+
+        @pl.when(k > 0)
+        def _():
+            copy.start()
+
+        return copy
+
+    def from_x(slots, sems):
+        for k in range(3):
+            pltpu.make_async_remote_copy(
+                src_ref=slots.at[k],
+                dst_ref=slots.at[k],
+                send_sem=send_sem.at[0],
+                recv_sem=sems.at[k],
+                device_id=sibling,
+                device_id_type=MESH,
+            ).wait_recv()
 
     def pair_done(px):
         for q, copy in enumerate(pairs[px]):
             copy.wait_recv()
             own = pl.ds(pl.multiple_of((px * 4 + q * 2 + core) * PIECE, 8), PIECE)
             pair_sum[px, q] = pair_sum[px, q] + grad[:, :, own, :]
-        k = (px - x + 4) % 4
-        slot = jnp.maximum(k - 1, 0)
-        n = net.count
-        net.count += 1
-        copy = pltpu.make_async_remote_copy(
-            src_ref=pair_sum.at[px, :, :, :, pl.ds(x0, xn)],
-            dst_ref=in1_x.at[slot],
-            send_sem=send_sem.at[n],
-            recv_sem=recv_x.at[slot],
-            device_id=device(px, y, z, core),
-            device_id_type=MESH,
-        )
-        first_x[px] = copy
-
-        @pl.when(k > 0)
-        def _():
-            copy.start()
+        first_x[px] = to_x(px, pair_sum.at[px, :, :, :, pl.ds(x0, xn)], in1_x, recv_x)
 
         for k in (1, 2, 3):
             ny = (y + k) % 4
-            first_y.append(
+            first_y.setdefault(px, []).append(
                 push(
                     pair_sum.at[px, :, :, ny, pl.ds(y0, yn)],
                     in1_y.at[k - 1, px],
@@ -427,7 +463,7 @@
             )
         for k in (1, 2, 3):
             nz = (z + k) % 4
-            first_z.append(
+            first_z.setdefault(px, []).append(
                 push(
                     pair_sum.at[px, nz % 2, nz // 2, :, pl.ds(z0, zn)],
                     in1_z.at[k - 1, px],
@@ -435,7 +471,30 @@
                 )
             )
 
+    second_y, sent_z = [], {}
+
+    def second_phase(px):
+        for copy in first_z[px]:
+            copy.wait_recv()
+        sum1_z[px] = (
+            pair_sum[px, zl, zh, :, pl.ds(z0, zn), :] + in1_z[0, px] + in1_z[1, px] + in1_z[2, px]
+        )
+        sent_z[px] = to_x(px, sum1_z.at[px], in2_z, recv_z)
+        for copy in first_y[px]:
+            copy.wait_recv()
+        sum1_y[px] = (
+            pair_sum[px, :, :, y, pl.ds(y0, yn), :] + in1_y[0, px] + in1_y[1, px] + in1_y[2, px]
+        )
+        for k in (1, 2, 3):
+            nz = (z + k) % 4
+            second_y.append(
+                push(
+                    sum1_y.at[px, nz % 2, nz // 2], in2_y.at[k - 1, px], device(x, y, nz, core)
+                )
+            )
+
     recv_x = recv_sem.at[pl.ds(RECV_X, 3)]
+    recv_z = recv_sem.at[pl.ds(RECV_X + 3, 3)]
     grad_second(3)
     pair_start(3)
     grad_second(2)
@@ -471,41 +530,22 @@
         lambda: smooth(gas_ref, halo, sm, (0, 7)),
         lambda: parcels(0),
         lambda: parcels(3),
+        parcel_store.start,
         lambda: deposit(0, cpair, hs, ob, dep),
-        lambda: deposit(3, cpair, hs, ob, dep),
-        send_deposit,
-    )
-
-    for k in (1, 2, 3):
-        pltpu.make_async_remote_copy(
-            src_ref=in1_x.at[k - 1],
-            dst_ref=in1_x.at[k - 1],
-            send_sem=send_sem.at[0],
-            recv_sem=recv_x.at[k - 1],
-            device_id=sibling,
-            device_id_type=MESH,
-        ).wait_recv()
+    )
+    second_phase(3)
+    second_phase(2)
+    when_evolving(lambda: deposit(3, cpair, hs, ob, dep), send_deposit)
+    second_phase(1)
+
+
+    from_x(in1_x, recv_x)
     sum1_x[...] = pair_sum[x, :, :, :, pl.ds(x0, xn), :] + in1_x[0] + in1_x[1] + in1_x[2]
     second_x = [
         push(sum1_x.at[:, :, (y + k) % 4], in2_x.at[k - 1], device(x, (y + k) % 4, z, core))
         for k in (1, 2, 3)
     ]
-    for copy in first_z:
-        copy.wait_recv()
-    sum1_z[...] = pair_sum[:, zl, zh, :, pl.ds(z0, zn), :] + in1_z[0] + in1_z[1] + in1_z[2]
-    second_z = [
-        push(sum1_z.at[(x + k) % 4], in2_z.at[k - 1], device((x + k) % 4, y, z, core))
-        for k in (1, 2, 3)
-    ]
-    for copy in first_y:
-        copy.wait_recv()
-    sum1_y[...] = pair_sum[:, :, :, y, pl.ds(y0, yn), :] + in1_y[0] + in1_y[1] + in1_y[2]
-    second_y = []
-    for k in (1, 2, 3):
-        nz = (z + k) % 4
-        second_y.append(
-            push(sum1_y.at[:, nz % 2, nz // 2], in2_y.at[k - 1], device(x, y, nz, core))
-        )
+    second_phase(0)
     for copy in second_x:
         copy.wait_recv()
     sum2_x[...] = sum1_x[:, :, y] + in2_x[0] + in2_x[1] + in2_x[2]
@@ -513,8 +553,7 @@
     for k in (1, 2, 3):
         nz = (z + k) % 4
         third_x.append(push(sum2_x.at[nz % 2, nz // 2], in3_x.at[k - 1], device(x, y, nz, core)))
-    for copy in second_z:
-        copy.wait_recv()
+    from_x(in2_z, recv_z)
     sum2_z[...] = sum1_z[x] + in2_z[0] + in2_z[1] + in2_z[2]
     third_z = [
         push(sum2_z.at[(y + k) % 4], in3_z.at[k - 1], device(x, (y + k) % 4, z, core))
@@ -538,25 +577,17 @@
         dep_low.wait,
         dep_high.wait,
         lambda: gas_second(gas_ref, halo, dep, dep_halo, gout_ref, mid),
-    )
-
-    @pl.when(jnp.logical_not(evo))
-    def _():
-        gout_ref[...] = gas_ref[...]
-        pout_ref[...] = pv_ref[...]
+        gas_store.start,
+    )
 
     for copy in across:
         copy.wait_recv()
     for j in range(8):
         flat[pl.ds(j, PIECE, stride=8), :] = fin[j]
-    gradient = flat[...]
-    first_new = BETA_ONE * m_ref[...] + (1.0 - BETA_ONE) * gradient
-    second_new = BETA_TWO * v_ref[...] + (1.0 - BETA_TWO) * gradient * gradient
-    mout_ref[...] = first_new
-    vout_ref[...] = second_new
-    first_hat = first_new / (1.0 - BETA_ONE**ADAM_STEP)
-    second_hat = second_new / (1.0 - BETA_TWO**ADAM_STEP)
-    wout_ref[...] = w_ref[...] - LEARN_RATE * first_hat / (jnp.sqrt(second_hat) + ADAM_EPS)
+    grad_store = pltpu.make_async_copy(flat, grad_out, out_sem.at[2])
+    grad_store.start()
+    for store in (gas_store, parcel_store, grad_store):
+        store.wait()
     for copy in sent:
         copy.wait_send()
     for px in range(4):
@@ -564,10 +595,43 @@
         @pl.when(px != x)
         def _():
             first_x[px].wait_send()
-
-
-def in_vmem(count):
-    return [pl.BlockSpec(memory_space=pltpu.VMEM)] * count
+            sent_z[px].wait_send()
+
+
+def finish_kernel(
+    grad_in, w_in, m_in, v_in, gas_in, parcel_in,
+    w_out, m_out, v_out, gas_out, parcel_out,
+    grad, w, m, v, gas, parcels, in_sem, out_sem,
+):
+    staged = (
+        (gas_in, gas), (parcel_in, parcels), (grad_in, grad), (m_in, m), (v_in, v), (w_in, w),
+    )
+    loads = [pltpu.make_async_copy(a, b, in_sem.at[i]) for i, (a, b) in enumerate(staged)]
+    results = ((gas, gas_out), (parcels, parcel_out), (m, m_out), (v, v_out), (w, w_out))
+    stores = [pltpu.make_async_copy(a, b, out_sem.at[i]) for i, (a, b) in enumerate(results)]
+    for load in loads:
+        load.start()
+    for n in range(2):
+        loads[n].wait()
+        stores[n].start()
+    for load in loads[2:]:
+        load.wait()
+    gradient = grad[...]
+    first_new = BETA_ONE * m[...] + (1.0 - BETA_ONE) * gradient
+    second_new = BETA_TWO * v[...] + (1.0 - BETA_TWO) * gradient * gradient
+    m[...] = first_new
+    v[...] = second_new
+    first_hat = first_new / (1.0 - BETA_ONE**ADAM_STEP)
+    second_hat = second_new / (1.0 - BETA_TWO**ADAM_STEP)
+    w[...] = w[...] - LEARN_RATE * first_hat / (jnp.sqrt(second_hat) + ADAM_EPS)
+    for store in stores[2:]:
+        store.start()
+    for store in stores:
+        store.wait()
+
+
+def anywhere(count):
+    return [pl.BlockSpec(memory_space=pl.ANY)] * count
 
 
 def shards(
@@ -575,13 +639,25 @@
     sample_blocks, learner_ids, master_weights, first_moment, second_moment,
 ):
     shape = jax.ShapeDtypeStruct
-    ids = jnp.broadcast_to(learner_ids[:, None], (BLK, 128))
     (_, _, xn), (_, _, yn), (_, _, zn) = PARTS
 
     def buf(*dims, dtype=F32):
         return pltpu.VMEM(dims, dtype)
 
     scratch = [
+        buf(BLK, 128, dtype=jnp.int32),
+        buf(640, 128),
+        buf(ROWS, 256, dtype=BF16),
+        buf(3, 8, 128, 128),
+        buf(3, 64, 1024),
+        buf(64, 1024, dtype=jnp.int32),
+        buf(1, 1024, dtype=jnp.int32),
+        buf(64, 1024),
+        buf(64, 1024),
+        buf(3, 8, 128, 128),
+        buf(3, 64, 1024),
+        pltpu.SemaphoreType.DMA((8,)),
+        pltpu.SemaphoreType.DMA((3,)),
         buf(8, 1280, 128, dtype=BF16),
         buf(3, 4, 128, 128),
         buf(5, 8, 128),
@@ -624,29 +700,42 @@
         buf(8, PIECE, 128),
         buf(640, 128),
         pltpu.SemaphoreType.DMA((RECV_X,)),
-        pltpu.SemaphoreType.DMA((RECV_X + 3,)),
+        pltpu.SemaphoreType.DMA((RECV_X + 6,)),
     ]
-    master_out, first_out, second_out, gas_out, parcels = pl.pallas_call(
+    grads, gas_out, parcels = pl.pallas_call(
         step_kernel,
         name="step",
         out_shape=(
             shape((640, 128), F32),
-            shape((640, 128), F32),
-            shape((640, 128), F32),
             shape((3, 8, 128, 128), F32),
             shape((3, 64, 1024), F32),
         ),
-        in_specs=in_vmem(11),
-        out_specs=tuple(in_vmem(5)),
+        in_specs=[pl.BlockSpec(memory_space=pltpu.SMEM)] + anywhere(8),
+        out_specs=tuple(anywhere(3)),
         scratch_shapes=scratch,
         compiler_params=pltpu.CompilerParams(
             collective_id=0, has_side_effects=True, vmem_limit_bytes=VMEM_LIMIT
         ),
     )(
-        master_weights, first_moment, second_moment, ids, sample_blocks.reshape(ROWS, 256),
-        gas_velocity[0], parcel_velocity[0], parcel_cell[0], block_fill, relax_rate[0],
-        parcel_mass[0],
-    )
+        learner_ids, master_weights, sample_blocks.reshape(ROWS, 256), gas_velocity[0],
+        parcel_velocity[0], parcel_cell[0], block_fill, relax_rate[0], parcel_mass[0],
+    )
+    state = shape((640, 128), F32)
+    master_out, first_out, second_out, gas_out, parcels = pl.pallas_call(
+        finish_kernel,
+        name="finish",
+        out_shape=(state, state, state, shape(gas_out.shape, F32), shape(parcels.shape, F32)),
+        in_specs=anywhere(6),
+        out_specs=tuple(anywhere(5)),
+        scratch_shapes=[buf(640, 128) for _ in range(4)]
+        + [
+            buf(*gas_out.shape),
+            buf(*parcels.shape),
+            pltpu.SemaphoreType.DMA((6,)),
+            pltpu.SemaphoreType.DMA((5,)),
+        ],
+        compiler_params=pltpu.CompilerParams(vmem_limit_bytes=VMEM_LIMIT),
+    )(grads, master_weights, first_moment, second_moment, gas_out, parcels)
     return gas_out[None], parcels[None], master_out, first_out, second_out
 
 

time: 85.8 us -> 71 us (0.83)
  local copies, waits for them, and re-layouts: 7.42 us -> 0 us
  Pallas kernels: 77.6 us -> 70.2 us
    pallas_call x1, Pallas kernels: 77.6 us -> 67 us  [shards(): pl.pallas_call(step_kernel, name='step', out_shape=(shape((640, 128), F32...]
    unnamed x13 -> x0, local copies, waits for them, and re-layouts: 6.09 us -> none
    pallas_call x0 -> x1, Pallas kernels: none -> 3.22 us  [shards(): pl.pallas_call(finish_kernel, name='finish', out_shape=(state, state, sta...]
    broadcast_in_dim x1 -> x0, local copies, waits for them, and re-layouts: 1.34 us -> none  [shards(): ids = jnp.broadcast_to(learner_ids[:, None], (BLK, 128))]
where the time goes in v3:
time: 71 us; the launch traced here: 70.8 us
  Pallas kernels  70.2 us (99%)
    pallas_call x1, Pallas kernels, shards(): pl.pallas_call(step_kernel, name='step', out_shape=(shape((640, 128), F32...  67 us
    pallas_call x1, Pallas kernels, shards(): pl.pallas_call(finish_kernel, name='finish', out_shape=(state, state, sta...  3.22 us

profile of v3, /device:TPU:0, one launch (start us, length us, event | category | flops | bytes accessed | tf_op | source)
XLA Modules:
  0.0 70.8 jit_solution(13854092322494571960)
XLA Ops:
  0.6 67.0 %step.1 = (f32[640,128]{1,0:T(8,128)}, f32[3,8,128,128]{3,2,1,0:T(8,128)}, f32[3,64,1024]{2,1,0:T(8,128)}) custom-call(s32[44]{0:T(128)} %ids_ref.1, f32[640,128]{1,0:T(8,128)} %w_in.3, bf16[704,256]{1,0:T(8,128)(2,1)} %bitcast.10, f32[3,8,128,128]{3,2,1,0:T(8,128)} %bitcast.8, f32[3,64,1024]{2,1,0:T(8,128)} %bitcast.9, s32[64,1024]{1,0:T(8,128)} %bitcast.11, ...), custom_call_target="tpu_custom_call" | custom-call | tf_op jit(solution)/shard_map/step/pallas_call | solution.py:705
  67.6 3.2 %finish.1 = (f32[640,128]{1,0:T(8,128)}, f32[640,128]{1,0:T(8,128)}, f32[640,128]{1,0:T(8,128)}, f32[3,8,128,128]{3,2,1,0:T(8,128)}, f32[3,64,1024]{2,1,0:T(8,128)}) custom-call(f32[640,128]{1,0:T(8,128)} %get-tuple-element.13.grad_in, f32[640,128]{1,0:T(8,128)} %w_in.3, f32[640,128]{1,0:T(8,128)} %m_in.1, f32[640,128]{1,0:T(8,128)} %v_in.1, ...), custom_call_target="tpu_custom_call" | custom-call | tf_op jit(solution)/shard_map/finish/pallas_call | solution.py:724

commit v4 on v3

--- a/solution.py
+++ b/solution.py
@@ -19,8 +19,7 @@
 BLK = 44
 ROWS = 704
 PIECE = 80
-PARTS = (("x", 0, 24), ("y", 24, 32), ("z", 56, 24))
-VMEM_LIMIT = 60 * 1024 * 1024
+VMEM_LIMIT = 46 * 1024 * 1024
 RECV_X = 150
 
 
@@ -202,13 +201,14 @@
 
 def step_kernel(
     ids_ref, w_in, xy_in, gas_in, pv_in, cell_in, fill_in, rate_in, mass_in,
-    grad_out, gas_out, parcel_out,
-    ids, w_ref, xy_ref, gas_ref, pv_ref, cell_ref, fill_ref, rate_ref, mass_ref, gout_ref, pout_ref,
+    flat, gout_ref, pout_ref,
+    ids, w_ref, xy_ref, gas_ref, pv_ref, cell_ref, fill_ref, rate_ref, mass_ref,
     in_sem, out_sem,
     wall, halo, cnt, cnt_in, sm, cpair, hs, ob, dep, dep_out, dep_halo, mid,
     a1, s1, a2, s2, b2, b1, err, w3f, w3, scale,
     grad, pair_sum, in1_x, in1_y, in1_z, sum1_x, sum1_y, sum1_z, in2_x, in2_y, in2_z,
-    sum2_x, sum2_y, sum2_z, in3_x, in3_y, in3_z, fin, flat, send_sem, recv_sem,
+    sum1_v, in2_v,
+    sum2_x, sum2_y, sum2_z, in3_x, in3_y, in3_z, fin, send_sem, recv_sem,
 ):
     x, y, z, core = coords()
     zh, zl = z // 2, z % 2
@@ -244,16 +244,16 @@
         load.start()
     for n in range(BLK):
         ids[pl.ds(n, 1), :] = jnp.full((1, 128), ids_ref[n], jnp.int32)
-    gas_store = pltpu.make_async_copy(gout_ref, gas_out, out_sem.at[0])
-    parcel_store = pltpu.make_async_copy(pout_ref, parcel_out, out_sem.at[1])
-    gas_same = pltpu.make_async_copy(gas_ref, gas_out, out_sem.at[0])
-    parcel_same = pltpu.make_async_copy(pv_ref, parcel_out, out_sem.at[1])
+    gas_same = pltpu.make_async_copy(gas_ref, gout_ref, out_sem.at[0])
+    parcel_same = pltpu.make_async_copy(pv_ref, pout_ref, out_sem.at[1])
 
     loads[0].wait()
     for j in range(8):
-        wall[j, pl.ds(pl.multiple_of(d * PIECE, 16), PIECE), :] = w_ref[
-            pl.ds(j, PIECE, stride=8), :
-        ].astype(BF16)
+        spread = w_ref[pl.ds(j, PIECE, stride=8), :]
+        mixed = jnp.concatenate([spread[:32], w_ref[pl.ds(256 + 48 * j, 48), :]], axis=0)
+        last = w_ref[pl.ds(PIECE * j, PIECE), :]
+        mine_j = jnp.where(d == 15, last, jnp.where(d == 14, mixed, spread))
+        wall[j, pl.ds(pl.multiple_of(d * PIECE, 16), PIECE), :] = mine_j.astype(BF16)
     lanes = lax.broadcasted_iota(jnp.int32, (BLK, 128), 1)
     mine = (ids[...] == lanes).astype(F32)
     cnt[0] = jnp.broadcast_to(jnp.sum(mine, axis=0, keepdims=True), (8, 128))
@@ -341,9 +341,8 @@
     when_evolving(low.start, high.start)
 
     for j in range(8):
-        w3f[pl.ds(j, 128, stride=8), :] = wall[j, pl.ds(1152, 128), :].astype(F32)
-    for i in range(4):
-        w3[i] = w3f[pl.ds(256 * i, 256), :].astype(BF16)
+        w3[pl.ds(48 * j, 48), :] = wall[j, pl.ds(1152, 48), :]
+        w3[pl.ds(384 + PIECE * j, PIECE), :] = wall[j, pl.ds(1200, PIECE), :]
 
     def columns(j, first, rows):
         return jnp.concatenate([wall[2 * j + i, pl.ds(first, rows), :] for i in range(2)], axis=1)
@@ -372,17 +371,19 @@
     for n in range(BLK):
         scale[pl.ds(16 * n, 16), :] = jnp.broadcast_to(per_block[n : n + 1], (16, 128))
     acts = jnp.concatenate([a2[i] for i in range(4)], axis=1)
-    predicted = dot(acts, jnp.concatenate([w3[i] for i in range(4)], axis=0))
+    predicted = dot(acts, w3[...])
     err[...] = ((predicted - xy_ref[:, 128:256].astype(F32)) * scale[...]).astype(BF16)
 
     def third_back(j, c):
-        w3f[pl.ds(pl.multiple_of(j * 256, 256), 256), :] = dot(a2[j], err[...], ((0,), (0,)))
-        b2[j] = (dot(err[...], w3[j], ((1,), (1,))) * s2[j]).astype(BF16)
+        part = pl.ds(pl.multiple_of(j * 256, 256), 256)
+        w3f[part, :] = dot(a2[j], err[...], ((0,), (0,)))
+        b2[j] = (dot(err[...], w3[part, :], ((1,), (1,))) * s2[j]).astype(BF16)
         return c
 
     lax.fori_loop(0, 4, third_back, 0)
     for j in range(8):
-        grad[j // 4, j % 4, pl.ds(1152, 128), :] = w3f[pl.ds(j, 128, stride=8), :]
+        grad[j // 4, j % 4, pl.ds(1152, 48), :] = w3f[pl.ds(48 * j, 48), :]
+        grad[j // 4, j % 4, pl.ds(1200, PIECE), :] = w3f[pl.ds(384 + PIECE * j, PIECE), :]
 
     def grad_second(i):
         for j in range(4):
@@ -398,7 +399,12 @@
         b1[i] = (dot(backs, rows, ((1,), (1,))) * s1[i]).astype(BF16)
         return c
 
-    (_, x0, xn), (_, y0, yn), (_, z0, zn) = PARTS
+    def y_rows(px):
+        return pl.ds(24, 32 if px % 2 else 24)
+
+    def z_rows(px):
+        return pl.ds(56, 24) if px % 2 else pl.ds(48, 32)
+
     pairs = {}
 
     def pair_start(px):
@@ -450,14 +456,14 @@
             copy.wait_recv()
             own = pl.ds(pl.multiple_of((px * 4 + q * 2 + core) * PIECE, 8), PIECE)
             pair_sum[px, q] = pair_sum[px, q] + grad[:, :, own, :]
-        first_x[px] = to_x(px, pair_sum.at[px, :, :, :, pl.ds(x0, xn)], in1_x, recv_x)
+        first_x[px] = to_x(px, pair_sum.at[px, :, :, :, pl.ds(0, 24)], in1_x, recv_x)
 
         for k in (1, 2, 3):
             ny = (y + k) % 4
             first_y.setdefault(px, []).append(
                 push(
-                    pair_sum.at[px, :, :, ny, pl.ds(y0, yn)],
-                    in1_y.at[k - 1, px],
+                    pair_sum.at[px, :, :, ny, y_rows(px)],
+                    in1_y.at[k - 1, px, :, :, pl.ds(0, y_rows(px).size)],
                     device(x, ny, z, core),
                 )
             )
@@ -465,36 +471,69 @@
             nz = (z + k) % 4
             first_z.setdefault(px, []).append(
                 push(
-                    pair_sum.at[px, nz % 2, nz // 2, :, pl.ds(z0, zn)],
-                    in1_z.at[k - 1, px],
+                    pair_sum.at[px, nz % 2, nz // 2, :, z_rows(px)],
+                    in1_z.at[k - 1, px, :, pl.ds(0, z_rows(px).size)],
                     device(x, y, nz, core),
                 )
             )
 
-    second_y, sent_z = [], {}
+    second_y, second_v, sent_z = {}, {}, {}
 
     def second_phase(px):
         for copy in first_z[px]:
             copy.wait_recv()
-        sum1_z[px] = (
-            pair_sum[px, zl, zh, :, pl.ds(z0, zn), :] + in1_z[0, px] + in1_z[1, px] + in1_z[2, px]
-        )
+        zn = z_rows(px).size
+        total = pair_sum[px, zl, zh, :, z_rows(px), :]
+        for k in range(3):
+            total = total + in1_z[k, px, :, pl.ds(0, zn), :]
+        sum1_z[px] = total[:, zn - 24 :]
         sent_z[px] = to_x(px, sum1_z.at[px], in2_z, recv_z)
+        if zn > 24:
+            sum1_v[px // 2] = total[:, :8]
+            second_v[px] = [
+                push(
+                    sum1_v.at[px // 2, (y + k) % 4],
+                    in2_v.at[k - 1, px // 2],
+                    device(x, (y + k) % 4, z, core),
+                )
+                for k in (1, 2, 3)
+            ]
         for copy in first_y[px]:
             copy.wait_recv()
-        sum1_y[px] = (
-            pair_sum[px, :, :, y, pl.ds(y0, yn), :] + in1_y[0, px] + in1_y[1, px] + in1_y[2, px]
-        )
+        yn = y_rows(px).size
+        total = pair_sum[px, :, :, y, y_rows(px), :]
+        for k in range(3):
+            total = total + in1_y[k, px, :, :, pl.ds(0, yn), :]
+        sum1_y[px, :, :, pl.ds(0, yn), :] = total
+        second_y[px] = []
         for k in (1, 2, 3):
             nz = (z + k) % 4
-            second_y.append(
+            second_y[px].append(
                 push(
-                    sum1_y.at[px, nz % 2, nz // 2], in2_y.at[k - 1, px], device(x, y, nz, core)
+                    sum1_y.at[px, nz % 2, nz // 2, pl.ds(0, yn)],
+                    in2_y.at[k - 1, px, pl.ds(0, yn)],
+                    device(x, y, nz, core),
                 )
             )
 
+    def third_phase(px):
+        for copy in second_y[px] + second_v.get(px, []):
+            copy.wait_recv()
+        yn = y_rows(px).size
+        rows = pl.ds(0, yn)
+        sum2_y[px, rows, :] = (
+            sum1_y[px, zl, zh, rows, :]
+            + in2_y[0, px, rows, :] + in2_y[1, px, rows, :] + in2_y[2, px, rows, :]
+        )
+        if yn == 24:
+            e = px // 2
+            sum2_y[px, pl.ds(24, 8), :] = sum1_v[e, y] + in2_v[0, e] + in2_v[1, e] + in2_v[2, e]
+        sent_y[px] = to_x(px, sum2_y.at[px], in3_y, recv_y)
+
+    sent_y = {}
     recv_x = recv_sem.at[pl.ds(RECV_X, 3)]
     recv_z = recv_sem.at[pl.ds(RECV_X + 3, 3)]
+    recv_y = recv_sem.at[pl.ds(RECV_X + 6, 3)]
     grad_second(3)
     pair_start(3)
     grad_second(2)
@@ -530,7 +569,6 @@
         lambda: smooth(gas_ref, halo, sm, (0, 7)),
         lambda: parcels(0),
         lambda: parcels(3),
-        parcel_store.start,
         lambda: deposit(0, cpair, hs, ob, dep),
     )
     second_phase(3)
@@ -540,7 +578,7 @@
 
 
     from_x(in1_x, recv_x)
-    sum1_x[...] = pair_sum[x, :, :, :, pl.ds(x0, xn), :] + in1_x[0] + in1_x[1] + in1_x[2]
+    sum1_x[...] = pair_sum[x, :, :, :, pl.ds(0, 24), :] + in1_x[0] + in1_x[1] + in1_x[2]
     second_x = [
         push(sum1_x.at[:, :, (y + k) % 4], in2_x.at[k - 1], device(x, (y + k) % 4, z, core))
         for k in (1, 2, 3)
@@ -559,35 +597,46 @@
         push(sum2_z.at[(y + k) % 4], in3_z.at[k - 1], device(x, (y + k) % 4, z, core))
         for k in (1, 2, 3)
     ]
-    for copy in second_y:
+    for px in (3, 2, 1, 0):
+        third_phase(px)
+    for copy in third_x + third_z:
         copy.wait_recv()
-    sum2_y[...] = sum1_y[:, zl, zh] + in2_y[0] + in2_y[1] + in2_y[2]
-    third_y = [
-        push(sum2_y.at[(x + k) % 4], in3_y.at[k - 1], device((x + k) % 4, y, z, core))
-        for k in (1, 2, 3)
-    ]
-    for copy in third_x + third_z + third_y:
-        copy.wait_recv()
-    fin[g, pl.ds(x0, xn), :] = sum2_x[zl, zh] + in3_x[0] + in3_x[1] + in3_x[2]
-    fin[g, pl.ds(y0, yn), :] = sum2_y[x] + in3_y[0] + in3_y[1] + in3_y[2]
-    fin[g, pl.ds(z0, zn), :] = sum2_z[y] + in3_z[0] + in3_z[1] + in3_z[2]
+    fin[g, pl.ds(0, 24), :] = sum2_x[zl, zh] + in3_x[0] + in3_x[1] + in3_x[2]
+    fin[g, pl.ds(56, 24), :] = sum2_z[y] + in3_z[0] + in3_z[1] + in3_z[2]
+    from_x(in3_y, recv_y)
+    fin[g, pl.ds(24, 32), :] = sum2_y[x] + in3_y[0] + in3_y[1] + in3_y[2]
     across = [push(fin.at[g], fin.at[g], ((g + k) % 8, d)) for k in range(1, 8)]
 
     when_evolving(
         dep_low.wait,
         dep_high.wait,
         lambda: gas_second(gas_ref, halo, dep, dep_halo, gout_ref, mid),
-        gas_store.start,
     )
 
     for copy in across:
         copy.wait_recv()
-    for j in range(8):
-        flat[pl.ds(j, PIECE, stride=8), :] = fin[j]
-    grad_store = pltpu.make_async_copy(flat, grad_out, out_sem.at[2])
-    grad_store.start()
-    for store in (gas_store, parcel_store, grad_store):
-        store.wait()
+
+    @pl.when(d < 14)
+    def _():
+        for j in range(8):
+            flat[pl.ds(j, PIECE, stride=8), :] = fin[j]
+
+    @pl.when(d == 14)
+    def _():
+        for j in range(8):
+            flat[pl.ds(j, 32, stride=8), :] = fin[j, :32]
+            flat[pl.ds(256 + 48 * j, 48), :] = fin[j, 32:]
+
+    @pl.when(d == 15)
+    def _():
+        for j in range(8):
+            flat[pl.ds(PIECE * j, PIECE), :] = fin[j]
+
+    @pl.when(jnp.logical_not(evo))
+    def _():
+        gas_same.wait()
+        parcel_same.wait()
+
     for copy in sent:
         copy.wait_send()
     for px in range(4):
@@ -596,34 +645,28 @@
         def _():
             first_x[px].wait_send()
             sent_z[px].wait_send()
+            sent_y[px].wait_send()
 
 
 def finish_kernel(
-    grad_in, w_in, m_in, v_in, gas_in, parcel_in,
+    grad, w, m, v, gas, parcels,
     w_out, m_out, v_out, gas_out, parcel_out,
-    grad, w, m, v, gas, parcels, in_sem, out_sem,
+    w_new, m_new, v_new, out_sem,
 ):
-    staged = (
-        (gas_in, gas), (parcel_in, parcels), (grad_in, grad), (m_in, m), (v_in, v), (w_in, w),
+    results = (
+        (gas, gas_out), (parcels, parcel_out), (m_new, m_out), (v_new, v_out), (w_new, w_out),
     )
-    loads = [pltpu.make_async_copy(a, b, in_sem.at[i]) for i, (a, b) in enumerate(staged)]
-    results = ((gas, gas_out), (parcels, parcel_out), (m, m_out), (v, v_out), (w, w_out))
     stores = [pltpu.make_async_copy(a, b, out_sem.at[i]) for i, (a, b) in enumerate(results)]
-    for load in loads:
-        load.start()
-    for n in range(2):
-        loads[n].wait()
-        stores[n].start()
-    for load in loads[2:]:
-        load.wait()
+    for store in stores[:2]:
+        store.start()
     gradient = grad[...]
     first_new = BETA_ONE * m[...] + (1.0 - BETA_ONE) * gradient
     second_new = BETA_TWO * v[...] + (1.0 - BETA_TWO) * gradient * gradient
-    m[...] = first_new
-    v[...] = second_new
+    m_new[...] = first_new
+    v_new[...] = second_new
     first_hat = first_new / (1.0 - BETA_ONE**ADAM_STEP)
     second_hat = second_new / (1.0 - BETA_TWO**ADAM_STEP)
-    w[...] = w[...] - LEARN_RATE * first_hat / (jnp.sqrt(second_hat) + ADAM_EPS)
+    w_new[...] = w[...] - LEARN_RATE * first_hat / (jnp.sqrt(second_hat) + ADAM_EPS)
     for store in stores[2:]:
         store.start()
     for store in stores:
@@ -639,7 +682,6 @@
     sample_blocks, learner_ids, master_weights, first_moment, second_moment,
 ):
     shape = jax.ShapeDtypeStruct
-    (_, _, xn), (_, _, yn), (_, _, zn) = PARTS
 
     def buf(*dims, dtype=F32):
         return pltpu.VMEM(dims, dtype)
@@ -654,10 +696,8 @@
         buf(1, 1024, dtype=jnp.int32),
         buf(64, 1024),
         buf(64, 1024),
-        buf(3, 8, 128, 128),
-        buf(3, 64, 1024),
         pltpu.SemaphoreType.DMA((8,)),
-        pltpu.SemaphoreType.DMA((3,)),
+        pltpu.SemaphoreType.DMA((2,)),
         buf(8, 1280, 128, dtype=BF16),
         buf(3, 4, 128, 128),
         buf(5, 8, 128),
@@ -678,63 +718,64 @@
         buf(4, ROWS, 256, dtype=BF16),
         buf(ROWS, 128, dtype=BF16),
         buf(1024, 128),
-        buf(4, 256, 128, dtype=BF16),
+        buf(1024, 128, dtype=BF16),
         buf(ROWS, 128),
         buf(2, 4, 1280, 128),
         buf(4, 2, 2, 4, PIECE, 128),
-        buf(3, 2, 2, 4, xn, 128),
-        buf(3, 4, 2, 2, yn, 128),
-        buf(3, 4, 4, zn, 128),
-        buf(2, 2, 4, xn, 128),
-        buf(4, 2, 2, yn, 128),
-        buf(4, 4, zn, 128),
-        buf(3, 2, 2, xn, 128),
-        buf(3, 4, yn, 128),
-        buf(3, 4, zn, 128),
-        buf(2, 2, xn, 128),
-        buf(4, yn, 128),
-        buf(4, zn, 128),
-        buf(3, xn, 128),
-        buf(3, yn, 128),
-        buf(3, zn, 128),
+        buf(3, 2, 2, 4, 24, 128),
+        buf(3, 4, 2, 2, 32, 128),
+        buf(3, 4, 4, 32, 128),
+        buf(2, 2, 4, 24, 128),
+        buf(4, 2, 2, 32, 128),
+        buf(4, 4, 24, 128),
+        buf(3, 2, 2, 24, 128),
+        buf(3, 4, 32, 128),
+        buf(3, 4, 24, 128),
+        buf(2, 4, 8, 128),
+        buf(3, 2, 8, 128),
+        buf(2, 2, 24, 128),
+        buf(4, 32, 128),
+        buf(4, 24, 128),
+        buf(3, 24, 128),
+        buf(3, 32, 128),
+        buf(3, 24, 128),
         buf(8, PIECE, 128),
-        buf(640, 128),
         pltpu.SemaphoreType.DMA((RECV_X,)),
-        pltpu.SemaphoreType.DMA((RECV_X + 6,)),
+        pltpu.SemaphoreType.DMA((RECV_X + 9,)),
     ]
     grads, gas_out, parcels = pl.pallas_call(
         step_kernel,
         name="step",
         out_shape=(
-            shape((640, 128), F32),
-            shape((3, 8, 128, 128), F32),
-            shape((3, 64, 1024), F32),
+            buf(640, 128),
+            buf(3, 8, 128, 128),
+            buf(3, 64, 1024),
         ),
-        in_specs=[pl.BlockSpec(memory_space=pltpu.SMEM)] + anywhere(8),
-        out_specs=tuple(anywhere(3)),
+        in_specs=[pl.BlockSpec(memory_space=pltpu.SMEM)]
+        + [pl.BlockSpec(memory_space=pltpu.HBM)] * 8,
+        out_specs=tuple([pl.BlockSpec(memory_space=pltpu.VMEM)] * 3),
         scratch_shapes=scratch,
         compiler_params=pltpu.CompilerParams(
             collective_id=0, has_side_effects=True, vmem_limit_bytes=VMEM_LIMIT
         ),
     )(
-        learner_ids, master_weights, sample_blocks.reshape(ROWS, 256), gas_velocity[0],
-        parcel_velocity[0], parcel_cell[0], block_fill, relax_rate[0], parcel_mass[0],
+        *[
+            pltpu.with_memory_space_constraint(array, pltpu.HBM)
+            for array in (
+                learner_ids, master_weights, sample_blocks.reshape(ROWS, 256), gas_velocity[0],
+                parcel_velocity[0], parcel_cell[0], block_fill, relax_rate[0], parcel_mass[0],
+            )
+        ],
     )
     state = shape((640, 128), F32)
     master_out, first_out, second_out, gas_out, parcels = pl.pallas_call(
         finish_kernel,
         name="finish",
         out_shape=(state, state, state, shape(gas_out.shape, F32), shape(parcels.shape, F32)),
-        in_specs=anywhere(6),
+        in_specs=[pl.BlockSpec(memory_space=pltpu.VMEM)] * 6,
         out_specs=tuple(anywhere(5)),
-        scratch_shapes=[buf(640, 128) for _ in range(4)]
-        + [
-            buf(*gas_out.shape),
-            buf(*parcels.shape),
-            pltpu.SemaphoreType.DMA((6,)),
-            pltpu.SemaphoreType.DMA((5,)),
-        ],
-        compiler_params=pltpu.CompilerParams(vmem_limit_bytes=VMEM_LIMIT),
+        scratch_shapes=[buf(640, 128) for _ in range(3)] + [pltpu.SemaphoreType.DMA((5,))],
+        compiler_params=pltpu.CompilerParams(vmem_limit_bytes=16 * 1024 * 1024),
     )(grads, master_weights, first_moment, second_moment, gas_out, parcels)
     return gas_out[None], parcels[None], master_out, first_out, second_out
 

time: 71 us -> 68.9 us (0.970)
  Pallas kernels: 70.2 us -> 68.1 us
    pallas_call x1, Pallas kernels: 3.22 us -> 1.76 us  [shards(): pl.pallas_call(finish_kernel, name='finish', out_shape=(state, state, sta...]
where the time goes in v4:
time: 68.9 us; the launch traced here: 68.8 us
  Pallas kernels  68.1 us (99%)
  between operations  0.69 us (1%)
    pallas_call x1, Pallas kernels, shards(): pl.pallas_call(step_kernel, name='step', out_shape=(buf(640, 128), buf(3,...  66.3 us
    pallas_call x1, Pallas kernels, shards(): pl.pallas_call(finish_kernel, name='finish', out_shape=(state, state, sta...  1.76 us

profile of v4, /device:TPU:0, one launch (start us, length us, event | category | flops | bytes accessed | tf_op | source)
XLA Modules:
  0.0 68.8 jit_solution(14719580917473022457)
XLA Ops:
  0.6 0.0 copy-start
  0.6 0.0 copy-start.1
  0.7 0.0 copy-start.2
  0.7 66.3 %step.1 = (f32[640,128]{1,0:T(8,128)S(1)}, f32[3,8,128,128]{3,2,1,0:T(8,128)S(1)}, f32[3,64,1024]{2,1,0:T(8,128)S(1)}) custom-call(s32[44]{0:T(128)} %ids_ref.1, f32[640,128]{1,0:T(8,128)} %w.1, bf16[704,256]{1,0:T(8,128)(2,1)} %bitcast.10, f32[3,8,128,128]{3,2,1,0:T(8,128)} %bitcast.8, f32[3,64,1024]{2,1,0:T(8,128)} %bitcast.9, s32[64,1024]{1,0:T(8,128)} %bitcast.11, ...), custom_call_target="tpu_custom_call" | custom-call | tf_op jit(solution)/shard_map/step/pallas_call | solution.py:746
  67.0 0.0 copy-done
  67.0 0.0 copy-done.1
  67.0 0.0 copy-done.2
  67.0 1.8 %finish.1 = (f32[640,128]{1,0:T(8,128)}, f32[640,128]{1,0:T(8,128)}, f32[640,128]{1,0:T(8,128)}, f32[3,8,128,128]{3,2,1,0:T(8,128)}, f32[3,64,1024]{2,1,0:T(8,128)}) custom-call(f32[640,128]{1,0:T(8,128)S(1)} %get-tuple-element.13.grad, f32[640,128]{1,0:T(8,128)S(1)} %copy-done, f32[640,128]{1,0:T(8,128)S(1)} %copy-done.1, f32[640,128]{1,0:T(8,128)S(1)} %copy-done.2, ...), custom_call_target="tpu_custom_call" | custom-call | tf_op jit(solution)/shard_map/finish/pallas_call | solution.py:771
Async XLA Ops:
  0.6 66.3 %copy-start = (f32[640,128]{1,0:T(8,128)S(1)}, f32[640,128]{1,0:T(8,128)}, u32[]{:S(2)}) copy-start(f32[640,128]{1,0:T(8,128)} %w.1) | copy-start | bytes 983044
  0.6 66.3 %copy-start.1 = (f32[640,128]{1,0:T(8,128)S(1)}, f32[640,128]{1,0:T(8,128)}, u32[]{:S(2)}) copy-start(f32[640,128]{1,0:T(8,128)} %m.1) | copy-start | bytes 983044
  0.7 66.3 %copy-start.2 = (f32[640,128]{1,0:T(8,128)S(1)}, f32[640,128]{1,0:T(8,128)}, u32[]{:S(2)}) copy-start(f32[640,128]{1,0:T(8,128)} %v.1) | copy-start | bytes 983044

commit v5 on v4

--- a/solution.py
+++ b/solution.py
@@ -339,7 +339,13 @@
         copy.wait_recv()
 
     when_evolving(low.start, high.start)
-
+    count_add(counting, 3, 7)
+
+    inverse = 1.0 / jnp.maximum(cnt[4, 0:1, :], 1.0)
+    picked = jnp.where(ids[...] == lanes, inverse, 0.0)
+    per_block = jnp.broadcast_to(jnp.sum(picked, axis=1, keepdims=True), (BLK, 128))
+    for n in range(BLK):
+        scale[pl.ds(16 * n, 16), :] = jnp.broadcast_to(per_block[n : n + 1], (16, 128))
     for j in range(8):
         w3[pl.ds(48 * j, 48), :] = wall[j, pl.ds(1152, 48), :]
         w3[pl.ds(384 + PIECE * j, PIECE), :] = wall[j, pl.ds(1200, PIECE), :]
@@ -353,34 +359,20 @@
         act[j] = value.astype(BF16)
         slope[j] = s + value * (1.0 - s)
 
-    def first(j, c):
+    for j in range(4):
         activate(dot(xy_ref[:, 0:128], columns(j, 0, 128)), a1, s1, j)
-        return c
-
-    def second(j, c):
-        acts = jnp.concatenate([a1[i] for i in range(4)], axis=1)
+    acts = jnp.concatenate([a1[i] for i in range(4)], axis=1)
+    for j in range(4):
         activate(dot(acts, columns(j, 128, 1024)), a2, s2, j)
-        return c
-
-    lax.fori_loop(0, 4, first, 0)
-    lax.fori_loop(0, 4, second, 0)
-    count_add(counting, 3, 7)
-    inverse = 1.0 / jnp.maximum(cnt[4, 0:1, :], 1.0)
-    picked = jnp.where(ids[...] == lanes, inverse, 0.0)
-    per_block = jnp.broadcast_to(jnp.sum(picked, axis=1, keepdims=True), (BLK, 128))
-    for n in range(BLK):
-        scale[pl.ds(16 * n, 16), :] = jnp.broadcast_to(per_block[n : n + 1], (16, 128))
     acts = jnp.concatenate([a2[i] for i in range(4)], axis=1)
     predicted = dot(acts, w3[...])
     err[...] = ((predicted - xy_ref[:, 128:256].astype(F32)) * scale[...]).astype(BF16)
 
-    def third_back(j, c):
-        part = pl.ds(pl.multiple_of(j * 256, 256), 256)
-        w3f[part, :] = dot(a2[j], err[...], ((0,), (0,)))
+    for j in range(4):
+        part = pl.ds(256 * j, 256)
         b2[j] = (dot(err[...], w3[part, :], ((1,), (1,))) * s2[j]).astype(BF16)
-        return c
-
-    lax.fori_loop(0, 4, third_back, 0)
+    for j in range(4):
+        w3f[pl.ds(256 * j, 256), :] = dot(a2[j], err[...], ((0,), (0,)))
     for j in range(8):
         grad[j // 4, j % 4, pl.ds(1152, 48), :] = w3f[pl.ds(48 * j, 48), :]
         grad[j // 4, j % 4, pl.ds(1200, PIECE), :] = w3f[pl.ds(384 + PIECE * j, PIECE), :]
@@ -392,18 +384,18 @@
                 n = 2 * j + e
                 grad[n // 4, n % 4, pl.ds(128 + 256 * i, 256), :] = piece[:, 128 * e : 128 * e + 128]
 
-    def back_first(i, c):
-        h0 = pl.multiple_of(128 + i * 256, 128)
+    def back_first():
         backs = jnp.concatenate([b2[j] for j in range(4)], axis=1)
-        rows = jnp.concatenate([wall[j, pl.ds(h0, 256), :] for j in range(8)], axis=1)
-        b1[i] = (dot(backs, rows, ((1,), (1,))) * s1[i]).astype(BF16)
-        return c
+        for i in range(4):
+            h0 = 128 + 256 * i
+            rows = jnp.concatenate([wall[j, pl.ds(h0, 256), :] for j in range(8)], axis=1)
+            b1[i] = (dot(backs, rows, ((1,), (1,))) * s1[i]).astype(BF16)
 
     def y_rows(px):
-        return pl.ds(24, 32 if px % 2 else 24)
+        return pl.ds(48, 32) if px % 2 else pl.ds(56, 24)
 
     def z_rows(px):
-        return pl.ds(56, 24) if px % 2 else pl.ds(48, 32)
+        return pl.ds(24, 24 if px % 2 else 32)
 
     pairs = {}
 
@@ -486,10 +478,10 @@
         total = pair_sum[px, zl, zh, :, z_rows(px), :]
         for k in range(3):
             total = total + in1_z[k, px, :, pl.ds(0, zn), :]
-        sum1_z[px] = total[:, zn - 24 :]
+        sum1_z[px] = total[:, :24]
         sent_z[px] = to_x(px, sum1_z.at[px], in2_z, recv_z)
         if zn > 24:
-            sum1_v[px // 2] = total[:, :8]
+            sum1_v[px // 2] = total[:, 24:]
             second_v[px] = [
                 push(
                     sum1_v.at[px // 2, (y + k) % 4],
@@ -521,13 +513,13 @@
             copy.wait_recv()
         yn = y_rows(px).size
         rows = pl.ds(0, yn)
-        sum2_y[px, rows, :] = (
+        sum2_y[px, pl.ds(32 - yn, yn), :] = (
             sum1_y[px, zl, zh, rows, :]
             + in2_y[0, px, rows, :] + in2_y[1, px, rows, :] + in2_y[2, px, rows, :]
         )
         if yn == 24:
             e = px // 2
-            sum2_y[px, pl.ds(24, 8), :] = sum1_v[e, y] + in2_v[0, e] + in2_v[1, e] + in2_v[2, e]
+            sum2_y[px, pl.ds(0, 8), :] = sum1_v[e, y] + in2_v[0, e] + in2_v[1, e] + in2_v[2, e]
         sent_y[px] = to_x(px, sum2_y.at[px], in3_y, recv_y)
 
     sent_y = {}
@@ -538,12 +530,12 @@
     pair_start(3)
     grad_second(2)
     pair_start(2)
+    grad_second(1)
     pair_done(3)
-    grad_second(1)
-    pair_done(2)
     grad_second(0)
     pair_start(1)
-    lax.fori_loop(0, 4, back_first, 0)
+    pair_done(2)
+    back_first()
     pair_done(1)
     for j in range(4):
         piece = dot(xy_ref[:, 0:128], b1[j], ((0,), (0,)))
@@ -602,11 +594,16 @@
     for copy in third_x + third_z:
         copy.wait_recv()
     fin[g, pl.ds(0, 24), :] = sum2_x[zl, zh] + in3_x[0] + in3_x[1] + in3_x[2]
-    fin[g, pl.ds(56, 24), :] = sum2_z[y] + in3_z[0] + in3_z[1] + in3_z[2]
+    fin[g, pl.ds(24, 24), :] = sum2_z[y] + in3_z[0] + in3_z[1] + in3_z[2]
+
+    def across_groups(rows):
+        return [
+            push(fin.at[g, rows], fin.at[g, rows], ((g + k) % 8, d)) for k in range(1, 8)
+        ]
+
     from_x(in3_y, recv_y)
-    fin[g, pl.ds(24, 32), :] = sum2_y[x] + in3_y[0] + in3_y[1] + in3_y[2]
-    across = [push(fin.at[g], fin.at[g], ((g + k) % 8, d)) for k in range(1, 8)]
-
+    fin[g, pl.ds(48, 32), :] = sum2_y[x] + in3_y[0] + in3_y[1] + in3_y[2]
+    across = across_groups(pl.ds(0, 80))
     when_evolving(
         dep_low.wait,
         dep_high.wait,

time: 68.9 us -> 65.3 us (0.948)
  Pallas kernels: 68.1 us -> 64.3 us
    pallas_call x1, Pallas kernels: 66.3 us -> 62.5 us  [shards(): pl.pallas_call(step_kernel, name='step', out_shape=(buf(640, 128), buf(3,...]
where the time goes in v5:
time: 65.3 us; the launch traced here: 65.2 us
  Pallas kernels  64.3 us (98%)
  between operations  0.85 us (1%)
    pallas_call x1, Pallas kernels, shards(): pl.pallas_call(step_kernel, name='step', out_shape=(buf(640, 128), buf(3,...  62.5 us
    pallas_call x1, Pallas kernels, shards(): pl.pallas_call(finish_kernel, name='finish', out_shape=(state, state, sta...  1.76 us

profile of v5, /device:TPU:0, one launch (start us, length us, event | category | flops | bytes accessed | tf_op | source)
XLA Modules:
  0.0 65.2 jit_solution(10168682343807751171)
XLA Ops:
  0.6 0.0 copy-start
  0.6 0.0 copy-start.1
  0.7 0.0 copy-start.2
  0.7 62.5 %step.1 = (f32[640,128]{1,0:T(8,128)S(1)}, f32[3,8,128,128]{3,2,1,0:T(8,128)S(1)}, f32[3,64,1024]{2,1,0:T(8,128)S(1)}) custom-call(s32[44]{0:T(128)} %ids_ref.1, f32[640,128]{1,0:T(8,128)} %w.1, bf16[704,256]{1,0:T(8,128)(2,1)} %bitcast.10, f32[3,8,128,128]{3,2,1,0:T(8,128)} %bitcast.8, f32[3,64,1024]{2,1,0:T(8,128)} %bitcast.9, s32[64,1024]{1,0:T(8,128)} %bitcast.11, ...), custom_call_target="tpu_custom_call" | custom-call | tf_op jit(solution)/shard_map/step/pallas_call | solution.py:743
  63.2 0.0 copy-done
  63.2 0.0 copy-done.1
  63.2 0.0 copy-done.2
  63.3 1.8 %finish.1 = (f32[640,128]{1,0:T(8,128)}, f32[640,128]{1,0:T(8,128)}, f32[640,128]{1,0:T(8,128)}, f32[3,8,128,128]{3,2,1,0:T(8,128)}, f32[3,64,1024]{2,1,0:T(8,128)}) custom-call(f32[640,128]{1,0:T(8,128)S(1)} %get-tuple-element.13.grad, f32[640,128]{1,0:T(8,128)S(1)} %copy-done, f32[640,128]{1,0:T(8,128)S(1)} %copy-done.1, f32[640,128]{1,0:T(8,128)S(1)} %copy-done.2, ...), custom_call_target="tpu_custom_call" | custom-call | tf_op jit(solution)/shard_map/finish/pallas_call | solution.py:768
Async XLA Ops:
  0.6 62.6 %copy-start = (f32[640,128]{1,0:T(8,128)S(1)}, f32[640,128]{1,0:T(8,128)}, u32[]{:S(2)}) copy-start(f32[640,128]{1,0:T(8,128)} %w.1) | copy-start | bytes 983044
  0.6 62.6 %copy-start.1 = (f32[640,128]{1,0:T(8,128)S(1)}, f32[640,128]{1,0:T(8,128)}, u32[]{:S(2)}) copy-start(f32[640,128]{1,0:T(8,128)} %m.1) | copy-start | bytes 983044
  0.7 62.6 %copy-start.2 = (f32[640,128]{1,0:T(8,128)S(1)}, f32[640,128]{1,0:T(8,128)}, u32[]{:S(2)}) copy-start(f32[640,128]{1,0:T(8,128)} %v.1) | copy-start | bytes 983044

commit v6 on v5

--- a/solution.py
+++ b/solution.py
@@ -208,7 +208,7 @@
     a1, s1, a2, s2, b2, b1, err, w3f, w3, scale,
     grad, pair_sum, in1_x, in1_y, in1_z, sum1_x, sum1_y, sum1_z, in2_x, in2_y, in2_z,
     sum1_v, in2_v,
-    sum2_x, sum2_y, sum2_z, in3_x, in3_y, in3_z, fin, send_sem, recv_sem,
+    sum2_x, sum2_y, sum2_z, in3_x, in3_y, in3_z, fin, spread_out, send_sem, recv_sem,
 ):
     x, y, z, core = coords()
     zh, zl = z // 2, z % 2
@@ -234,7 +234,7 @@
     for partner in partners:
         pl.semaphore_signal(barrier, inc=1, device_id=partner, device_id_type=MESH)
     pairs_in = (
-        (w_in, w_ref), (gas_in, gas_ref), (cell_in, cell_ref), (pv_in, pv_ref), (rate_in, rate_ref),
+        (w_in, w_ref.at[pl.ds(0, 640)]), (gas_in, gas_ref), (cell_in, cell_ref), (pv_in, pv_ref), (rate_in, rate_ref),
         (mass_in, mass_ref), (fill_in, fill_ref), (xy_in, xy_ref),
     )
     loads = [
@@ -616,7 +616,8 @@
     @pl.when(d < 14)
     def _():
         for j in range(8):
-            flat[pl.ds(j, PIECE, stride=8), :] = fin[j]
+            spread_out[pl.ds(j, PIECE, stride=8), :] = fin[j]
+        flat[...] = spread_out[pl.ds(0, 640), :]
 
     @pl.when(d == 14)
     def _():
@@ -685,7 +686,7 @@
 
     scratch = [
         buf(BLK, 128, dtype=jnp.int32),
-        buf(640, 128),
+        buf(648, 128),
         buf(ROWS, 256, dtype=BF16),
         buf(3, 8, 128, 128),
         buf(3, 64, 1024),
@@ -701,8 +702,8 @@
         buf(10, 8, 128),
         buf(3, 1024, 128),
         buf(512, 128, dtype=jnp.int32),
-        buf(8192, 128),
-        buf(4096, 128),
+        buf(8208, 128),
+        buf(4112, 128),
         buf(3, 1024, 128),
         buf(2, 3, 2, 128, 128, dtype=BF16),
         buf(2, 3, 2, 128, 128, dtype=BF16),
@@ -737,6 +738,7 @@
         buf(3, 32, 128),
         buf(3, 24, 128),
         buf(8, PIECE, 128),
+        buf(648, 128),
         pltpu.SemaphoreType.DMA((RECV_X,)),
         pltpu.SemaphoreType.DMA((RECV_X + 9,)),
     ]

time: 65.3 us -> 65.3 us (level)
  no operation moved by 1% of the time
where the time goes in v6:
time: 65.3 us; the launch traced here: 65.2 us
  Pallas kernels  64.3 us (98%)
  between operations  0.85 us (1%)
    pallas_call x1, Pallas kernels, shards(): pl.pallas_call(step_kernel, name='step', out_shape=(buf(640, 128), buf(3,...  62.5 us
    pallas_call x1, Pallas kernels, shards(): pl.pallas_call(finish_kernel, name='finish', out_shape=(state, state, sta...  1.76 us

profile of v6, /device:TPU:0, one launch (start us, length us, event | category | flops | bytes accessed | tf_op | source)
XLA Modules:
  0.0 65.2 jit_solution(5124432620195814066)
XLA Ops:
  0.6 0.0 copy-start
  0.6 0.0 copy-start.1
  0.7 0.0 copy-start.2
  0.7 62.5 %step.1 = (f32[640,128]{1,0:T(8,128)S(1)}, f32[3,8,128,128]{3,2,1,0:T(8,128)S(1)}, f32[3,64,1024]{2,1,0:T(8,128)S(1)}) custom-call(s32[44]{0:T(128)} %ids_ref.1, f32[640,128]{1,0:T(8,128)} %w.1, bf16[704,256]{1,0:T(8,128)(2,1)} %bitcast.10, f32[3,8,128,128]{3,2,1,0:T(8,128)} %bitcast.8, f32[3,64,1024]{2,1,0:T(8,128)} %bitcast.9, s32[64,1024]{1,0:T(8,128)} %bitcast.11, ...), custom_call_target="tpu_custom_call" | custom-call | tf_op jit(solution)/shard_map/step/pallas_call | solution.py:745
  63.2 0.0 copy-done
  63.2 0.0 copy-done.1
  63.2 0.0 copy-done.2
  63.2 1.8 %finish.1 = (f32[640,128]{1,0:T(8,128)}, f32[640,128]{1,0:T(8,128)}, f32[640,128]{1,0:T(8,128)}, f32[3,8,128,128]{3,2,1,0:T(8,128)}, f32[3,64,1024]{2,1,0:T(8,128)}) custom-call(f32[640,128]{1,0:T(8,128)S(1)} %get-tuple-element.13.grad, f32[640,128]{1,0:T(8,128)S(1)} %copy-done, f32[640,128]{1,0:T(8,128)S(1)} %copy-done.1, f32[640,128]{1,0:T(8,128)S(1)} %copy-done.2, ...), custom_call_target="tpu_custom_call" | custom-call | tf_op jit(solution)/shard_map/finish/pallas_call | solution.py:770
Async XLA Ops:
  0.6 62.6 %copy-start = (f32[640,128]{1,0:T(8,128)S(1)}, f32[640,128]{1,0:T(8,128)}, u32[]{:S(2)}) copy-start(f32[640,128]{1,0:T(8,128)} %w.1) | copy-start | bytes 983044
  0.6 62.6 %copy-start.1 = (f32[640,128]{1,0:T(8,128)S(1)}, f32[640,128]{1,0:T(8,128)}, u32[]{:S(2)}) copy-start(f32[640,128]{1,0:T(8,128)} %m.1) | copy-start | bytes 983044
  0.7 62.6 %copy-start.2 = (f32[640,128]{1,0:T(8,128)S(1)}, f32[640,128]{1,0:T(8,128)}, u32[]{:S(2)}) copy-start(f32[640,128]{1,0:T(8,128)} %v.1) | copy-start | bytes 983044

commit v7 on v6

--- a/solution.py
+++ b/solution.py
@@ -531,9 +531,9 @@
     grad_second(2)
     pair_start(2)
     grad_second(1)
-    pair_done(3)
     grad_second(0)
     pair_start(1)
+    pair_done(3)
     pair_done(2)
     back_first()
     pair_done(1)
@@ -566,7 +566,6 @@
     second_phase(3)
     second_phase(2)
     when_evolving(lambda: deposit(3, cpair, hs, ob, dep), send_deposit)
-    second_phase(1)
 
 
     from_x(in1_x, recv_x)
@@ -575,6 +574,7 @@
         push(sum1_x.at[:, :, (y + k) % 4], in2_x.at[k - 1], device(x, (y + k) % 4, z, core))
         for k in (1, 2, 3)
     ]
+    second_phase(1)
     second_phase(0)
     for copy in second_x:
         copy.wait_recv()

time: 65.3 us -> 65.4 us (level)
  no operation moved by 1% of the time
where the time goes in v7:
time: 65.4 us; the launch traced here: 65.2 us
  Pallas kernels  64.4 us (98%)
  between operations  0.85 us (1%)
    pallas_call x1, Pallas kernels, shards(): pl.pallas_call(step_kernel, name='step', out_shape=(buf(640, 128), buf(3,...  62.6 us
    pallas_call x1, Pallas kernels, shards(): pl.pallas_call(finish_kernel, name='finish', out_shape=(state, state, sta...  1.76 us

profile of v7, /device:TPU:0, one launch (start us, length us, event | category | flops | bytes accessed | tf_op | source)
XLA Modules:
  0.0 65.2 jit_solution(8119866508838367549)
XLA Ops:
  0.6 0.0 copy-start
  0.6 0.0 copy-start.1
  0.7 0.0 copy-start.2
  0.7 62.6 %step.1 = (f32[640,128]{1,0:T(8,128)S(1)}, f32[3,8,128,128]{3,2,1,0:T(8,128)S(1)}, f32[3,64,1024]{2,1,0:T(8,128)S(1)}) custom-call(s32[44]{0:T(128)} %ids_ref.1, f32[640,128]{1,0:T(8,128)} %w.1, bf16[704,256]{1,0:T(8,128)(2,1)} %bitcast.10, f32[3,8,128,128]{3,2,1,0:T(8,128)} %bitcast.8, f32[3,64,1024]{2,1,0:T(8,128)} %bitcast.9, s32[64,1024]{1,0:T(8,128)} %bitcast.11, ...), custom_call_target="tpu_custom_call" | custom-call | tf_op jit(solution)/shard_map/step/pallas_call | solution.py:745
  63.3 0.0 copy-done
  63.3 0.0 copy-done.1
  63.3 0.0 copy-done.2
  63.3 1.8 %finish.1 = (f32[640,128]{1,0:T(8,128)}, f32[640,128]{1,0:T(8,128)}, f32[640,128]{1,0:T(8,128)}, f32[3,8,128,128]{3,2,1,0:T(8,128)}, f32[3,64,1024]{2,1,0:T(8,128)}) custom-call(f32[640,128]{1,0:T(8,128)S(1)} %get-tuple-element.13.grad, f32[640,128]{1,0:T(8,128)S(1)} %copy-done, f32[640,128]{1,0:T(8,128)S(1)} %copy-done.1, f32[640,128]{1,0:T(8,128)S(1)} %copy-done.2, ...), custom_call_target="tpu_custom_call" | custom-call | tf_op jit(solution)/shard_map/finish/pallas_call | solution.py:770
Async XLA Ops:
  0.6 62.6 %copy-start = (f32[640,128]{1,0:T(8,128)S(1)}, f32[640,128]{1,0:T(8,128)}, u32[]{:S(2)}) copy-start(f32[640,128]{1,0:T(8,128)} %w.1) | copy-start | bytes 983044
  0.6 62.6 %copy-start.1 = (f32[640,128]{1,0:T(8,128)S(1)}, f32[640,128]{1,0:T(8,128)}, u32[]{:S(2)}) copy-start(f32[640,128]{1,0:T(8,128)} %m.1) | copy-start | bytes 983044
  0.7 62.6 %copy-start.2 = (f32[640,128]{1,0:T(8,128)S(1)}, f32[640,128]{1,0:T(8,128)}, u32[]{:S(2)}) copy-start(f32[640,128]{1,0:T(8,128)} %v.1) | copy-start | bytes 983044
